TPU v7x, 32 devices: a whole 2x2x4 slice. The times are simulated.
32 devices in a mesh: groups: 2 (over y), rows: 4 (over x, core), cols: 4 (over z).
Axes of the slice: x: 2, y: 2, z: 4, core: 2. Of those that a mesh axis runs over, the one named last changes fastest.
Arguments:
- contact_map: bfloat16 [128, 64, 128], P(('groups', 'rows'), 'cols'), parts along dimension 0, may hold values from -6 to 6
- w_near: bfloat16 [2, 3, 3, 128, 128], replicated, may hold values from -0.1875 to 0.1875
- w_far: bfloat16 [2, 3, 3, 128, 128], replicated, may hold values from -0.1875 to 0.1875
Outputs:
- refined_map: bfloat16 [128, 64, 128], P(('groups', 'rows'), 'cols'), parts along dimension 0
There are 2 independent parts, one for each index of `groups`. A program takes and returns all parts, laid end to end along the dimension named above; an argument that names none is the same for every part. Nothing has to cross between parts.
All inputs are finite; a program needn't handle non-finite values.
Results may differ from a plain program's by a relative error of at most 0.0066.
Values may be sent and summed in bfloat16 or wider, within the bound.
A program may use at most 64 MiB of HBM per device.

v0:
```python
import jax
import jax.numpy as jnp
from jax import lax
from jax.sharding import PartitionSpec as P


def extended(cells, sides, width):
    for axis, dim in sides:
        count = lax.axis_size(axis)
        ends = count - 1
        head = lax.slice_in_dim(cells, 0, width, axis=dim)
        tail = lax.slice_in_dim(cells, cells.shape[dim] - width, cells.shape[dim], axis=dim)
        cells = jnp.concatenate(
            [
                lax.ppermute(tail, axis, [(i, (i + 1) % count) for i in range(ends)]),
                cells,
                lax.ppermute(head, axis, [((i + 1) % count, i) for i in range(ends)]),
            ],
            axis=dim,
        )
    return cells


def valid_conv(padded, kernel, spread):
    out = lax.conv_general_dilated(
        padded[None],
        kernel,
        (1, 1),
        "VALID",
        rhs_dilation=(spread, spread),
        dimension_numbers=("NHWC", "HWIO", "NHWC"),
        preferred_element_type=jnp.float32,
    )
    return out[0]


def average(block_out, mirrored):
    flipped = jnp.swapaxes(mirrored, 0, 1)
    return ((block_out.astype(jnp.float32) + flipped.astype(jnp.float32)) * 0.5).astype(
        jnp.bfloat16
    )


def on_device(contact_map, w_near, w_far):
    blocks = w_near.shape[0]
    state = lax.all_to_all(contact_map, "cols", split_axis=0, concat_axis=1, tiled=True)
    for block in range(blocks):
        padded = extended(state, ((("rows", "cols"), 0),), 2)
        padded = jnp.pad(padded, ((0, 0), (2, 2), (0, 0)))
        hidden = jax.nn.relu(valid_conv(padded, w_near[block], 2)).astype(jnp.bfloat16)
        padded = extended(hidden, ((("rows", "cols"), 0),), 4)
        padded = jnp.pad(padded, ((0, 0), (4, 4), (0, 0)))
        block_out = (state.astype(jnp.float32) + valid_conv(padded, w_far[block], 4)).astype(
            jnp.bfloat16
        )
        mirrored = lax.all_to_all(
            block_out, ("rows", "cols"), split_axis=1, concat_axis=0, tiled=True
        )
        state = average(block_out, mirrored)
    return lax.all_to_all(state, "cols", split_axis=1, concat_axis=0, tiled=True)


def solution(mesh):
    in_specs = (P(("groups", "rows"), "cols", None), P(), P())
    out_specs = P(("groups", "rows"), "cols", None)
    return jax.shard_map(
        on_device, mesh=mesh, in_specs=in_specs, out_specs=out_specs, check_vma=False
    )
```

profile of v0, /device:TPU:0, one launch (start us, length us, event | category | flops | bytes accessed | tf_op | source)
XLA Modules:
  0.0 87.5 jit_solution(11584903854671900995)
XLA Ops:
  0.0 12.1 %all_to_all.54 = bf16[16,16,128]{2,1,0:T(8,128)(2,1)S(1)} all-to-all(bf16[16,16,128]{2,1,0:T(8,128)(2,1)} %param.3), channel_id=1, replica_groups=mesh['groups'=2,'rows'=4,'cols'=4] {'cols'}, dimensions={0} | all-to-all | bytes 131072 | tf_op jit(solution)/shard_map/all_to_all | solution.py:46
  12.1 1.3 %collective-permute-start.1 = (bf16[2,64,128]{2,1,0:T(8,128)(2,1)S(1)}, bf16[2,64,128]{2,1,0:T(8,128)(2,1)S(1)}, u32[]{:S(2)}, u32[]{:S(2)}) collective-permute-start(bf16[2,64,128]{2,1,0:T(8,128)(2,1)S(1)} %bitcast.94), channel_id=1, source_target_pairs={{1,0},{2,1},{3,2},{4,3},{5,4},{6,5},{7,6},{8,7},{9,8},{10,9},{11,1... | collective-permute-start | bytes 98312 | tf_op jit(solution)/shard_map/ppermute | solution.py:17
  13.4 4.5 %collective-permute-start = (bf16[2,64,128]{2,1,0:T(8,128)(2,1)S(1)}, bf16[2,64,128]{2,1,0:T(8,128)(2,1)S(1)}, u32[]{:S(2)}, u32[]{:S(2)}) collective-permute-start(bf16[2,64,128]{2,1,0:T(8,128)(2,1)S(1)} %bitcast.93), channel_id=1, source_target_pairs={{0,1},{1,2},{2,3},{3,4},{4,5},{5,6},{6,7},{7,8},{8,9},{9,10},{10,1... | collective-permute-start | bytes 98312 | tf_op jit(solution)/shard_map/ppermute | solution.py:15
  18.0 0.0 collective-permute-done.1
  18.0 1.6 %collective-permute-done = bf16[2,64,128]{2,1,0:T(8,128)(2,1)S(1)} collective-permute-done((bf16[2,64,128]{2,1,0:T(8,128)(2,1)S(1)}, bf16[2,64,128]{2,1,0:T(8,128)(2,1)S(1)}, u32[]{:S(2)}, u32[]{:S(2)}) %collective-permute-start) | collective-permute-done | bytes 32800 | tf_op jit(solution)/shard_map/ppermute | solution.py:15
  19.5 0.0 copy-start
  19.7 0.0 copy-start.2
  19.7 0.9 %copy-done = bf16[2,3,3,128,128]{4,3,2,1,0:T(8,128)(2,1)S(1)} copy-done((bf16[2,3,3,128,128]{4,3,2,1,0:T(8,128)(2,1)S(1)}, bf16[2,3,3,128,128]{4,3,2,1,0:T(8,128)(2,1)}, u32[]{:S(2)}) %copy-start) | copy-done | bytes 589848
  20.6 0.0 copy-done.2
  20.6 0.3 fusion.2
  21.0 0.0 copy-start.1
  21.0 1.4 %collective-permute-start.3 = (bf16[4,64,128]{2,0,1:T(4,128)(2,1)S(1)}, bf16[4,64,128]{2,0,1:T(4,128)(2,1)S(1)}, u32[]{:S(2)}, u32[]{:S(2)}) collective-permute-start(bf16[4,64,128]{2,0,1:T(4,128)(2,1)S(1)} %slice_bitcast_fusion.1), channel_id=1, source_target_pairs={{1,0},{2,1},{3,2},{4,3},{5,4},{6,5},{7,6},{8,7},{9,8},{10,9},{11,1... | collective-permute-start | bytes 196616 | tf_op jit(solution)/shard_map/ppermute | solution.py:17
  22.5 4.9 %collective-permute-start.2 = (bf16[4,64,128]{2,0,1:T(4,128)(2,1)S(1)}, bf16[4,64,128]{2,0,1:T(4,128)(2,1)S(1)}, u32[]{:S(2)}, u32[]{:S(2)}) collective-permute-start(bf16[4,64,128]{2,0,1:T(4,128)(2,1)S(1)} %slice_bitcast_fusion.1), channel_id=1, source_target_pairs={{0,1},{1,2},{2,3},{3,4},{4,5},{5,6},{6,7},{7,8},{8,9},{9,10},{10,1... | collective-permute-start | bytes 196616 | tf_op jit(solution)/shard_map/ppermute | solution.py:15
  27.3 0.3 collective-permute-done.3
  27.6 1.6 %collective-permute-done.2 = bf16[4,64,128]{2,0,1:T(4,128)(2,1)S(1)} collective-permute-done((bf16[4,64,128]{2,0,1:T(4,128)(2,1)S(1)}, bf16[4,64,128]{2,0,1:T(4,128)(2,1)S(1)}, u32[]{:S(2)}, u32[]{:S(2)}) %collective-permute-start.2) | collective-permute-done | bytes 65568 | tf_op jit(solution)/shard_map/ppermute | solution.py:15
  29.2 0.1 select_maximum_fusion.2
  29.3 0.1 copy.54
  29.4 0.1 slice.52
  29.5 0.0 copy-done.1
  29.5 0.3 convolution_select_fusion.2
  29.9 0.1 copy.57
  30.0 14.2 %all_to_all.55 = bf16[4,64,128]{2,0,1:T(4,128)(2,1)S(1)} all-to-all(bf16[4,64,128]{2,0,1:T(4,128)(2,1)S(1)} %copy.57), channel_id=1, replica_groups=mesh['groups'=2,'rows'=4,'cols'=4] {'rows','cols'}, dimensions={1} | all-to-all | bytes 131072 | tf_op jit(solution)/shard_map/all_to_all | solution.py:56
  44.2 2.2 %collective-permute-start.4 = (bf16[2,64,128]{2,1,0:T(8,128)(2,1)S(1)}, bf16[2,64,128]{2,1,0:T(8,128)(2,1)S(1)}, u32[]{:S(2)}, u32[]{:S(2)}) collective-permute-start(bf16[2,64,128]{2,1,0:T(8,128)(2,1)S(1)} %get-tuple-element.5), channel_id=1, source_target_pairs={{0,1},{1,2},{2,3},{3,4},{4,5},{5,6},{6,7},{7,8},{8,9},{9,10},{10,1... | collective-permute-start | bytes 98312 | tf_op jit(solution)/shard_map/ppermute | solution.py:15
  46.5 1.3 %collective-permute-start.5 = (bf16[2,64,128]{2,1,0:T(8,128)(2,1)S(1)}, bf16[2,64,128]{2,1,0:T(8,128)(2,1)S(1)}, u32[]{:S(2)}, u32[]{:S(2)}) collective-permute-start(bf16[2,64,128]{2,1,0:T(8,128)(2,1)S(1)} %get-tuple-element.6), channel_id=1, source_target_pairs={{1,0},{2,1},{3,2},{4,3},{5,4},{6,5},{7,6},{8,7},{9,8},{10,9},{11,1... | collective-permute-start | bytes 98312 | tf_op jit(solution)/shard_map/ppermute | solution.py:17
  47.8 0.3 collective-permute-done.4
  48.0 4.2 %collective-permute-done.5 = bf16[2,64,128]{2,1,0:T(8,128)(2,1)S(1)} collective-permute-done((bf16[2,64,128]{2,1,0:T(8,128)(2,1)S(1)}, bf16[2,64,128]{2,1,0:T(8,128)(2,1)S(1)}, u32[]{:S(2)}, u32[]{:S(2)}) %collective-permute-start.5) | collective-permute-done | bytes 32800 | tf_op jit(solution)/shard_map/ppermute | solution.py:17
  52.4 0.3 fusion.3
  52.9 1.3 %collective-permute-start.7 = (bf16[4,64,128]{2,0,1:T(4,128)(2,1)S(1)}, bf16[4,64,128]{2,0,1:T(4,128)(2,1)S(1)}, u32[]{:S(2)}, u32[]{:S(2)}) collective-permute-start(bf16[4,64,128]{2,0,1:T(4,128)(2,1)S(1)} %slice_bitcast_fusion), channel_id=1, source_target_pairs={{1,0},{2,1},{3,2},{4,3},{5,4},{6,5},{7,6},{8,7},{9,8},{10,9},{11,1... | collective-permute-start | bytes 196616 | tf_op jit(solution)/shard_map/ppermute | solution.py:17
  54.2 4.5 %collective-permute-start.6 = (bf16[4,64,128]{2,0,1:T(4,128)(2,1)S(1)}, bf16[4,64,128]{2,0,1:T(4,128)(2,1)S(1)}, u32[]{:S(2)}, u32[]{:S(2)}) collective-permute-start(bf16[4,64,128]{2,0,1:T(4,128)(2,1)S(1)} %slice_bitcast_fusion), channel_id=1, source_target_pairs={{0,1},{1,2},{2,3},{3,4},{4,5},{5,6},{6,7},{7,8},{8,9},{9,10},{10,1... | collective-permute-start | bytes 196616 | tf_op jit(solution)/shard_map/ppermute | solution.py:15
  58.7 0.5 collective-permute-done.7
  59.2 1.9 %collective-permute-done.6 = bf16[4,64,128]{2,0,1:T(4,128)(2,1)S(1)} collective-permute-done((bf16[4,64,128]{2,0,1:T(4,128)(2,1)S(1)}, bf16[4,64,128]{2,0,1:T(4,128)(2,1)S(1)}, u32[]{:S(2)}, u32[]{:S(2)}) %collective-permute-start.6) | collective-permute-done | bytes 65568 | tf_op jit(solution)/shard_map/ppermute | solution.py:15
  61.1 0.1 select_maximum_fusion
  61.2 0.1 copy.64
  61.3 0.1 slice.58
  61.4 0.3 convolution_select_fusion
  61.8 0.1 copy.67
  61.9 16.7 %all_to_all.56 = bf16[4,64,128]{2,0,1:T(4,128)(2,1)S(1)} all-to-all(bf16[4,64,128]{2,0,1:T(4,128)(2,1)S(1)} %copy.67), channel_id=1, replica_groups=mesh['groups'=2,'rows'=4,'cols'=4] {'rows','cols'}, dimensions={1} | all-to-all | bytes 131072 | tf_op jit(solution)/shard_map/all_to_all | solution.py:56
  78.7 0.1 copy.69
  78.7 8.1 %all_to_all.57 = bf16[4,64,128]{2,0,1:T(4,128)(2,1)S(1)} all-to-all(bf16[4,64,128]{2,0,1:T(4,128)(2,1)S(1)} %copy.69), channel_id=1, replica_groups=mesh['groups'=2,'rows'=4,'cols'=4] {'cols'}, dimensions={1} | all-to-all | bytes 131072 | tf_op jit(solution)/shard_map/all_to_all | solution.py:60
  86.8 0.6 copy.71
  (30 shorter events, 0.6 us)
Async XLA Ops:
  12.1 5.9 %collective-permute-start.1 = (bf16[2,64,128]{2,1,0:T(8,128)(2,1)S(1)}, bf16[2,64,128]{2,1,0:T(8,128)(2,1)S(1)}, u32[]{:S(2)}, u32[]{:S(2)}) collective-permute-start(bf16[2,64,128]{2,1,0:T(8,128)(2,1)S(1)} %bitcast.94), channel_id=1, source_target_pairs={{1,0},{2,1},{3,2},{4,3},{5,4},{6,5},{7,6},{8,7},{9,8},{10,9},{11,1... | collective-permute-start | bytes 98312 | tf_op jit(solution)/shard_map/ppermute | solution.py:17
  13.4 6.1 %collective-permute-start = (bf16[2,64,128]{2,1,0:T(8,128)(2,1)S(1)}, bf16[2,64,128]{2,1,0:T(8,128)(2,1)S(1)}, u32[]{:S(2)}, u32[]{:S(2)}) collective-permute-start(bf16[2,64,128]{2,1,0:T(8,128)(2,1)S(1)} %bitcast.93), channel_id=1, source_target_pairs={{0,1},{1,2},{2,3},{3,4},{4,5},{5,6},{6,7},{7,8},{8,9},{9,10},{10,1... | collective-permute-start | bytes 98312 | tf_op jit(solution)/shard_map/ppermute | solution.py:15
  19.5 1.1 %copy-start = (bf16[2,3,3,128,128]{4,3,2,1,0:T(8,128)(2,1)S(1)}, bf16[2,3,3,128,128]{4,3,2,1,0:T(8,128)(2,1)}, u32[]{:S(2)}) copy-start(bf16[2,3,3,128,128]{4,3,2,1,0:T(8,128)(2,1)} %param.4) | copy-start | bytes 1769476
  19.7 0.9 %copy-start.2 = (pred[8,9]{0,1:T(8,128)(4,1)S(1)}, pred[8,9]{0,1:T(8,128)(4,1)}, u32[]{:S(2)}) copy-start(pred[8,9]{0,1:T(8,128)(4,1)} %constant.31) | copy-start | bytes 220
  21.0 8.5 %copy-start.1 = (bf16[2,3,3,128,128]{4,3,2,1,0:T(8,128)(2,1)S(1)}, bf16[2,3,3,128,128]{4,3,2,1,0:T(8,128)(2,1)}, u32[]{:S(2)}) copy-start(bf16[2,3,3,128,128]{4,3,2,1,0:T(8,128)(2,1)} %param.5) | copy-start | bytes 1769476
  21.0 6.6 %collective-permute-start.3 = (bf16[4,64,128]{2,0,1:T(4,128)(2,1)S(1)}, bf16[4,64,128]{2,0,1:T(4,128)(2,1)S(1)}, u32[]{:S(2)}, u32[]{:S(2)}) collective-permute-start(bf16[4,64,128]{2,0,1:T(4,128)(2,1)S(1)} %slice_bitcast_fusion.1), channel_id=1, source_target_pairs={{1,0},{2,1},{3,2},{4,3},{5,4},{6,5},{7,6},{8,7},{9,8},{10,9},{11,1... | collective-permute-start | bytes 196616 | tf_op jit(solution)/shard_map/ppermute | solution.py:17
  22.5 6.7 %collective-permute-start.2 = (bf16[4,64,128]{2,0,1:T(4,128)(2,1)S(1)}, bf16[4,64,128]{2,0,1:T(4,128)(2,1)S(1)}, u32[]{:S(2)}, u32[]{:S(2)}) collective-permute-start(bf16[4,64,128]{2,0,1:T(4,128)(2,1)S(1)} %slice_bitcast_fusion.1), channel_id=1, source_target_pairs={{0,1},{1,2},{2,3},{3,4},{4,5},{5,6},{6,7},{7,8},{8,9},{9,10},{10,1... | collective-permute-start | bytes 196616 | tf_op jit(solution)/shard_map/ppermute | solution.py:15
  44.2 3.8 %collective-permute-start.4 = (bf16[2,64,128]{2,1,0:T(8,128)(2,1)S(1)}, bf16[2,64,128]{2,1,0:T(8,128)(2,1)S(1)}, u32[]{:S(2)}, u32[]{:S(2)}) collective-permute-start(bf16[2,64,128]{2,1,0:T(8,128)(2,1)S(1)} %get-tuple-element.5), channel_id=1, source_target_pairs={{0,1},{1,2},{2,3},{3,4},{4,5},{5,6},{6,7},{7,8},{8,9},{9,10},{10,1... | collective-permute-start | bytes 98312 | tf_op jit(solution)/shard_map/ppermute | solution.py:15
  46.5 5.8 %collective-permute-start.5 = (bf16[2,64,128]{2,1,0:T(8,128)(2,1)S(1)}, bf16[2,64,128]{2,1,0:T(8,128)(2,1)S(1)}, u32[]{:S(2)}, u32[]{:S(2)}) collective-permute-start(bf16[2,64,128]{2,1,0:T(8,128)(2,1)S(1)} %get-tuple-element.6), channel_id=1, source_target_pairs={{1,0},{2,1},{3,2},{4,3},{5,4},{6,5},{7,6},{8,7},{9,8},{10,9},{11,1... | collective-permute-start | bytes 98312 | tf_op jit(solution)/shard_map/ppermute | solution.py:17
  52.9 6.3 %collective-permute-start.7 = (bf16[4,64,128]{2,0,1:T(4,128)(2,1)S(1)}, bf16[4,64,128]{2,0,1:T(4,128)(2,1)S(1)}, u32[]{:S(2)}, u32[]{:S(2)}) collective-permute-start(bf16[4,64,128]{2,0,1:T(4,128)(2,1)S(1)} %slice_bitcast_fusion), channel_id=1, source_target_pairs={{1,0},{2,1},{3,2},{4,3},{5,4},{6,5},{7,6},{8,7},{9,8},{10,9},{11,1... | collective-permute-start | bytes 196616 | tf_op jit(solution)/shard_map/ppermute | solution.py:17
  54.2 6.9 %collective-permute-start.6 = (bf16[4,64,128]{2,0,1:T(4,128)(2,1)S(1)}, bf16[4,64,128]{2,0,1:T(4,128)(2,1)S(1)}, u32[]{:S(2)}, u32[]{:S(2)}) collective-permute-start(bf16[4,64,128]{2,0,1:T(4,128)(2,1)S(1)} %slice_bitcast_fusion), channel_id=1, source_target_pairs={{0,1},{1,2},{2,3},{3,4},{4,5},{5,6},{6,7},{7,8},{8,9},{9,10},{10,1... | collective-permute-start | bytes 196616 | tf_op jit(solution)/shard_map/ppermute | solution.py:15
where the time goes:
time: 88 us; the launch traced here: 87.5 us
  blocking collectives  51.1 us (58%)
  starting transfers between devices  21.5 us (24%)
  waiting for transfers between devices  10.3 us (12%)
  local copies, waits for them, and re-layouts  2.37 us (3%)
  matrix products  1.38 us (2%)
    all_to_all x2, blocking collectives, on_device(): lax.all_to_all(block_out, ('rows', 'cols'), split_axis=1, concat_axis=0,...  30.9 us
    ppermute x4, starting transfers between devices, extended(): lax.ppermute(tail, axis, [(i, (i + 1) % count) for i in range(ends)])  16.2 us
    all_to_all x1, blocking collectives, on_device(): lax.all_to_all(contact_map, 'cols', split_axis=0, concat_axis=1, tiled=True)  12.1 us
    all_to_all x1, blocking collectives, on_device(): lax.all_to_all(state, 'cols', split_axis=1, concat_axis=0, tiled=True)  8.11 us
    ppermute x4, waiting for transfers between devices, extended(): lax.ppermute(tail, axis, [(i, (i + 1) % count) for i in range(ends)])  5.31 us
    ppermute x4, starting transfers between devices, extended(): lax.ppermute(head, axis, [((i + 1) % count, i) for i in range(ends)])  5.3 us
    ppermute x4, waiting for transfers between devices, extended(): lax.ppermute(head, axis, [((i + 1) % count, i) for i in range(ends)])  5.01 us
  transfers between devices with their start and end apart: 8, of which 7 were waited for; matrix products, arithmetic and copies ran while one was open for 0% of the time, Pallas kernels for 0%

commit v1 on v0

--- a/solution.py
+++ b/solution.py
@@ -1,7 +1,17 @@
+import functools
+
 import jax
 import jax.numpy as jnp
 from jax import lax
+from jax.experimental import pallas as pl
+from jax.experimental.pallas import tpu as pltpu
 from jax.sharding import PartitionSpec as P
+
+MESH = pl.DeviceIdType.MESH
+NEAR, FAR = 2, 4
+HALO = NEAR + FAR
+PAD = 16
+SIDES = [(-1, 0), (1, 0), (0, -1), (0, 1), (-1, -1), (-1, 1), (1, -1), (1, 1)]
 
 
 def extended(cells, sides, width):
@@ -34,30 +44,256 @@
     return out[0]
 
 
-def average(block_out, mirrored):
-    flipped = jnp.swapaxes(mirrored, 0, 1)
+def average(block_out, flipped):
     return ((block_out.astype(jnp.float32) + flipped.astype(jnp.float32)) * 0.5).astype(
         jnp.bfloat16
     )
 
 
-def on_device(contact_map, w_near, w_far):
+def by_rows(contact_map, w_near, w_far):
     blocks = w_near.shape[0]
     state = lax.all_to_all(contact_map, "cols", split_axis=0, concat_axis=1, tiled=True)
     for block in range(blocks):
-        padded = extended(state, ((("rows", "cols"), 0),), 2)
-        padded = jnp.pad(padded, ((0, 0), (2, 2), (0, 0)))
-        hidden = jax.nn.relu(valid_conv(padded, w_near[block], 2)).astype(jnp.bfloat16)
-        padded = extended(hidden, ((("rows", "cols"), 0),), 4)
-        padded = jnp.pad(padded, ((0, 0), (4, 4), (0, 0)))
-        block_out = (state.astype(jnp.float32) + valid_conv(padded, w_far[block], 4)).astype(
+        padded = extended(state, ((("rows", "cols"), 0),), NEAR)
+        padded = jnp.pad(padded, ((0, 0), (NEAR, NEAR), (0, 0)))
+        hidden = jax.nn.relu(valid_conv(padded, w_near[block], NEAR)).astype(jnp.bfloat16)
+        padded = extended(hidden, ((("rows", "cols"), 0),), FAR)
+        padded = jnp.pad(padded, ((0, 0), (FAR, FAR), (0, 0)))
+        block_out = (state.astype(jnp.float32) + valid_conv(padded, w_far[block], FAR)).astype(
             jnp.bfloat16
         )
         mirrored = lax.all_to_all(
             block_out, ("rows", "cols"), split_axis=1, concat_axis=0, tiled=True
         )
-        state = average(block_out, mirrored)
+        state = average(block_out, jnp.swapaxes(mirrored, 0, 1))
     return lax.all_to_all(state, "cols", split_axis=1, concat_axis=0, tiled=True)
+
+
+def flip(cells):
+    return jnp.transpose(cells, (1, 0, 2))
+
+
+def tile_kernel(
+    count, side, x_ref, near_ref, far_ref, out_ref,
+    pads, turned, strips, mirror, near, far, load_sem, send_sem, recv_sem, mirror_sem,
+):
+    blocks, channels = near_ref.shape[0], near_ref.shape[-1]
+    row, col = lax.axis_index("rows"), lax.axis_index("cols")
+    last = count - 1
+    inner = slice(HALO, HALO + side)
+    body = slice(PAD, PAD + side)
+
+    load = pltpu.make_async_copy(x_ref, pads.at[0, inner, body], load_sem.at[0])
+    load.start()
+    load_near = pltpu.make_async_copy(near_ref, near, load_sem.at[1])
+    load_far = pltpu.make_async_copy(far_ref, far, load_sem.at[2])
+    load_near.start()
+    load_far.start()
+
+    def there(step):
+        di, dj = step
+        ok = []
+        if di:
+            ok.append(row > 0 if di < 0 else row < last)
+        if dj:
+            ok.append(col > 0 if dj < 0 else col < last)
+        return ok[0] if len(ok) == 1 else jnp.logical_and(*ok)
+
+    barrier = pltpu.get_barrier_semaphore()
+    friends = jnp.int32(0)
+    for step in SIDES:
+        yes = there(step)
+        friends += yes.astype(jnp.int32)
+
+        @pl.when(yes)
+        def _():
+            pl.semaphore_signal(
+                barrier, inc=1, device_id={"rows": row + step[0], "cols": col + step[1]},
+                device_id_type=MESH,
+            )
+
+    @pl.when(row != col)
+    def _():
+        pl.semaphore_signal(
+            barrier, inc=1, device_id={"rows": col, "cols": row}, device_id_type=MESH
+        )
+
+    friends += (row != col).astype(jnp.int32)
+
+    zero = functools.partial(jnp.zeros, dtype=jnp.bfloat16)
+    wide = pads.shape[2]
+    for n in range(blocks):
+        @pl.when(row == 0)
+        def _():
+            pads[n, :HALO] = zero((HALO, wide, channels))
+
+        @pl.when(row == last)
+        def _():
+            pads[n, HALO + side:] = zero((HALO, wide, channels))
+
+        @pl.when(col == 0)
+        def _():
+            pads[n, :, :PAD] = zero((side + 2 * HALO, PAD, channels))
+
+        @pl.when(col == last)
+        def _():
+            pads[n, :, PAD + side:] = zero((side + 2 * HALO, PAD, channels))
+
+    load.wait()
+    pl.semaphore_wait(barrier, friends)
+
+    def rim_copy(n, at):
+        di, dj = SIDES[at]
+        if di:
+            rows = slice(HALO, 2 * HALO) if di < 0 else slice(side, side + HALO)
+            to = slice(HALO + side, 2 * HALO + side) if di < 0 else slice(0, HALO)
+            start = PAD - dj * side
+            source = pads.at[n, rows, body]
+            target = pads.at[n, to, start:start + side]
+        else:
+            source = turned.at[n, 0 if dj < 0 else 1]
+            target = strips.at[n, 1 if dj < 0 else 0]
+        return pltpu.make_async_remote_copy(
+            src_ref=source, dst_ref=target,
+            send_sem=send_sem.at[n, at], recv_sem=recv_sem.at[n, at],
+            device_id={"rows": row + di, "cols": col + dj}, device_id_type=MESH,
+        )
+
+    def rim(n):
+        flat = flip(pads[n, inner, body])
+        turned[n, 0] = flat[:HALO]
+        turned[n, 1] = flat[side - HALO:]
+        for at, step in enumerate(SIDES):
+            @pl.when(there(step))
+            def _():
+                rim_copy(n, at).start()
+
+    def rim_wait(n):
+        for at, (di, dj) in enumerate(SIDES):
+            @pl.when(there((-di, -dj)))
+            def _():
+                rim_copy(n, at).wait_recv()
+
+        @pl.when(col > 0)
+        def _():
+            pads[n, inner, PAD - HALO:PAD] = flip(strips[n, 0])
+
+        @pl.when(col < last)
+        def _():
+            pads[n, inner, PAD + side:PAD + side + HALO] = flip(strips[n, 1])
+
+    reach = side + 2 * FAR
+    span = side + PAD
+
+    def hidden_of(n, weights):
+        first = PAD - HALO
+        taps = [
+            pads[n, NEAR * a:NEAR * a + reach, first + NEAR * b:first + NEAR * b + span]
+            .reshape(reach * span, channels)
+            for a in range(3) for b in range(3)
+        ]
+        total = jnp.dot(
+            jnp.concatenate(taps, axis=1), weights, preferred_element_type=jnp.float32
+        )
+        total = jnp.maximum(total, 0.0).reshape(reach, span, total.shape[-1])
+        i = lax.broadcasted_iota(jnp.int32, total.shape, 0) + (row * side - FAR)
+        j = lax.broadcasted_iota(jnp.int32, total.shape, 1) + (col * side - FAR)
+        whole = count * side
+        on_map = (i >= 0) & (i < whole) & (j >= 0) & (j < whole)
+        return jnp.where(on_map, total, 0.0).astype(jnp.bfloat16)
+
+    def block_out_of(n, hidden, weights):
+        taps = [
+            hidden[FAR * a:FAR * a + side, FAR * b:FAR * b + side]
+            .reshape(side * side, channels)
+            for a in range(3) for b in range(3)
+        ]
+        total = jnp.dot(
+            jnp.concatenate(taps, axis=1), weights, preferred_element_type=jnp.float32
+        ).reshape(side, side, channels)
+        return (pads[n, inner, body].astype(jnp.float32) + total).astype(jnp.bfloat16)
+
+    def straight(w, n):
+        return w[n].reshape(9 * channels, channels)
+
+    def crossed(w, n):
+        return jnp.concatenate([w[n, b, a] for a in range(3) for b in range(3)], axis=0)
+
+    rim(0)
+    load_near.wait()
+    load_far.wait()
+    for n in range(blocks - 1):
+        rim_wait(n)
+        hidden = hidden_of(n, straight(near, n))
+        block_out = block_out_of(n, hidden, straight(far, n))
+        mirror[n, 0] = flip(block_out)
+        swap = pltpu.make_async_remote_copy(
+            src_ref=mirror.at[n, 0], dst_ref=mirror.at[n, 1],
+            send_sem=mirror_sem.at[n, 0], recv_sem=mirror_sem.at[n, 1],
+            device_id={"rows": col, "cols": row}, device_id_type=MESH,
+        )
+
+        @pl.when(row != col)
+        def _():
+            swap.start()
+            swap.wait()
+
+        @pl.when(row == col)
+        def _():
+            mirror[n, 1] = mirror[n, 0]
+
+        pads[n + 1, inner, body] = average(block_out, mirror[n, 1])
+        rim(n + 1)
+
+    n = blocks - 1
+    both = jnp.concatenate([straight(near, n), crossed(near, n)], axis=1)
+    rim_wait(n)
+    hidden = hidden_of(n, both)
+    block_out = block_out_of(n, hidden[..., :channels], straight(far, n))
+    flipped = block_out_of(n, hidden[..., channels:], crossed(far, n))
+    out_ref[...] = average(block_out, flipped)
+
+    for n in range(blocks):
+        for at, step in enumerate(SIDES):
+            @pl.when(there(step))
+            def _():
+                rim_copy(n, at).wait_send()
+
+
+def by_tiles(contact_map, w_near, w_far):
+    blocks, channels = w_near.shape[0], w_near.shape[-1]
+    side, count = contact_map.shape[0], lax.axis_size("rows")
+    kind = contact_map.dtype
+    anywhere = pl.BlockSpec(memory_space=pl.ANY)
+    return pl.pallas_call(
+        functools.partial(tile_kernel, count, side),
+        out_shape=jax.ShapeDtypeStruct(contact_map.shape, kind),
+        in_specs=[anywhere] * 3,
+        out_specs=pl.BlockSpec(memory_space=pltpu.VMEM),
+        scratch_shapes=[
+            pltpu.VMEM((blocks, side + 2 * HALO, side + 2 * PAD, channels), kind),
+            pltpu.VMEM((blocks, 2, HALO, side, channels), kind),
+            pltpu.VMEM((blocks, 2, HALO, side, channels), kind),
+            pltpu.VMEM((blocks, 2, side, side, channels), kind),
+            pltpu.VMEM(w_near.shape, kind),
+            pltpu.VMEM(w_far.shape, kind),
+            pltpu.SemaphoreType.DMA((3,)),
+            pltpu.SemaphoreType.DMA((blocks, len(SIDES))),
+            pltpu.SemaphoreType.DMA((blocks, len(SIDES))),
+            pltpu.SemaphoreType.DMA((blocks, 2)),
+        ],
+        compiler_params=pltpu.CompilerParams(
+            collective_id=0, has_side_effects=True, vmem_limit_bytes=32 * 2**20
+        ),
+    )(contact_map, w_near, w_far)
+
+
+def on_device(contact_map, w_near, w_far):
+    side = contact_map.shape[0]
+    square = side == contact_map.shape[1] and side % PAD == 0
+    if square and lax.axis_size("rows") == lax.axis_size("cols") and w_near.shape[0] > 1:
+        return by_tiles(contact_map, w_near, w_far)
+    return by_rows(contact_map, w_near, w_far)
 
 
 def solution(mesh):

time: 88 us -> 23.6 us (0.27)
  the two profiles are of different devices: /device:TPU:0 before, /device:TPU:1 now
where the time goes in v1:
time: 23.6 us; the launch traced here: 23.4 us
  Pallas kernels  19.7 us (83%)
  local copies, waits for them, and re-layouts  3.6 us (15%)
    pallas_call x1, Pallas kernels, by_tiles(): pl.pallas_call(functools.partial(tile_kernel, count, side), out_shape=jax...  19.7 us
    unnamed x7, local copies, waits for them, and re-layouts  3.6 us

profile of v1, /device:TPU:1, one launch (start us, length us, event | category | flops | bytes accessed | tf_op | source)
XLA Modules:
  0.0 23.4 jit_solution(10146463314957326430)
XLA Ops:
  0.0 0.0 copy-start
  0.0 1.1 %copy-done = bf16[2,3,3,128,128]{4,3,2,1,0:T(8,128)(2,1)S(1)} copy-done((bf16[2,3,3,128,128]{4,3,2,1,0:T(8,128)(2,1)S(1)}, bf16[2,3,3,128,128]{4,3,2,1,0:T(8,128)(2,1)}, u32[]{:S(2)}) %copy-start) | copy-done | bytes 589848
  1.1 0.0 copy-start.1
  1.1 1.1 %copy-done.1 = bf16[2,3,3,128,128]{4,3,2,1,0:T(8,128)(2,1)S(1)} copy-done((bf16[2,3,3,128,128]{4,3,2,1,0:T(8,128)(2,1)S(1)}, bf16[2,3,3,128,128]{4,3,2,1,0:T(8,128)(2,1)}, u32[]{:S(2)}) %copy-start.1) | copy-done | bytes 589848
  2.1 0.0 copy-start.2
  2.1 0.8 %copy-done.2 = bf16[16,16,128]{2,1,0:T(8,128)(2,1)S(1)} copy-done((bf16[16,16,128]{2,1,0:T(8,128)(2,1)S(1)}, bf16[16,16,128]{2,1,0:T(8,128)(2,1)}, u32[]{:S(2)}) %copy-start.2) | copy-done | bytes 65560
  3.0 19.7 %shard_map.37 = bf16[16,16,128]{2,1,0:T(8,128)(2,1)S(1)} custom-call(bf16[16,16,128]{2,1,0:T(8,128)(2,1)S(1)} %copy-done.2, bf16[2,3,3,128,128]{4,3,2,1,0:T(8,128)(2,1)S(1)} %copy-done, bf16[2,3,3,128,128]{4,3,2,1,0:T(8,128)(2,1)S(1)} %copy-done.1), custom_call_target="tpu_custom_call" | custom-call | tf_op jit(solution)/shard_map/pallas_call | solution.py:268
  22.7 0.6 %copy.5 = bf16[16,16,128]{2,1,0:T(8,128)(2,1)} copy(bf16[16,16,128]{2,1,0:T(8,128)(2,1)S(1)} %shard_map.37) | data formatting | bytes 131072
Async XLA Ops:
  0.0 1.1 %copy-start = (bf16[2,3,3,128,128]{4,3,2,1,0:T(8,128)(2,1)S(1)}, bf16[2,3,3,128,128]{4,3,2,1,0:T(8,128)(2,1)}, u32[]{:S(2)}) copy-start(bf16[2,3,3,128,128]{4,3,2,1,0:T(8,128)(2,1)} %near_ref.1) | copy-start | bytes 1769476
  1.1 1.1 %copy-start.1 = (bf16[2,3,3,128,128]{4,3,2,1,0:T(8,128)(2,1)S(1)}, bf16[2,3,3,128,128]{4,3,2,1,0:T(8,128)(2,1)}, u32[]{:S(2)}) copy-start(bf16[2,3,3,128,128]{4,3,2,1,0:T(8,128)(2,1)} %far_ref.1) | copy-start | bytes 1769476
  2.1 0.8 %copy-start.2 = (bf16[16,16,128]{2,1,0:T(8,128)(2,1)S(1)}, bf16[16,16,128]{2,1,0:T(8,128)(2,1)}, u32[]{:S(2)}) copy-start(bf16[16,16,128]{2,1,0:T(8,128)(2,1)} %x_ref.1) | copy-start | bytes 196612

commit v2 on v1

v2 whole, which is shorter than its diff:
```python
import functools

import jax
import jax.numpy as jnp
from jax import lax
from jax.experimental import pallas as pl
from jax.experimental.pallas import tpu as pltpu
from jax.sharding import PartitionSpec as P

MESH = pl.DeviceIdType.MESH
NEAR, FAR = 2, 4
HALO = NEAR + FAR
PAD, PACK = 16, 8
SIDES = [(0, -1), (0, 1), (-1, -1), (-1, 1), (1, -1), (1, 1), (-1, 0), (1, 0)]


def extended(cells, sides, width):
    for axis, dim in sides:
        count = lax.axis_size(axis)
        ends = count - 1
        head = lax.slice_in_dim(cells, 0, width, axis=dim)
        tail = lax.slice_in_dim(cells, cells.shape[dim] - width, cells.shape[dim], axis=dim)
        cells = jnp.concatenate(
            [
                lax.ppermute(tail, axis, [(i, (i + 1) % count) for i in range(ends)]),
                cells,
                lax.ppermute(head, axis, [((i + 1) % count, i) for i in range(ends)]),
            ],
            axis=dim,
        )
    return cells


def valid_conv(padded, kernel, spread):
    out = lax.conv_general_dilated(
        padded[None],
        kernel,
        (1, 1),
        "VALID",
        rhs_dilation=(spread, spread),
        dimension_numbers=("NHWC", "HWIO", "NHWC"),
        preferred_element_type=jnp.float32,
    )
    return out[0]


def average(block_out, flipped):
    return ((block_out.astype(jnp.float32) + flipped.astype(jnp.float32)) * 0.5).astype(
        jnp.bfloat16
    )


def by_rows(contact_map, w_near, w_far):
    blocks = w_near.shape[0]
    state = lax.all_to_all(contact_map, "cols", split_axis=0, concat_axis=1, tiled=True)
    for block in range(blocks):
        padded = extended(state, ((("rows", "cols"), 0),), NEAR)
        padded = jnp.pad(padded, ((0, 0), (NEAR, NEAR), (0, 0)))
        hidden = jax.nn.relu(valid_conv(padded, w_near[block], NEAR)).astype(jnp.bfloat16)
        padded = extended(hidden, ((("rows", "cols"), 0),), FAR)
        padded = jnp.pad(padded, ((0, 0), (FAR, FAR), (0, 0)))
        block_out = (state.astype(jnp.float32) + valid_conv(padded, w_far[block], FAR)).astype(
            jnp.bfloat16
        )
        mirrored = lax.all_to_all(
            block_out, ("rows", "cols"), split_axis=1, concat_axis=0, tiled=True
        )
        state = average(block_out, jnp.swapaxes(mirrored, 0, 1))
    return lax.all_to_all(state, "cols", split_axis=1, concat_axis=0, tiled=True)


def flip(cells):
    return jnp.transpose(cells, (1, 0, 2))


def tile_kernel(
    count, side, x_ref, near_ref, far_ref, out_ref,
    pads, turned, strips, corners, mirror, hidden, near, far,
    load_sem, send_sem, recv_sem, mirror_sem,
):
    blocks, channels = near_ref.shape[0], near_ref.shape[-1]
    row, col = lax.axis_index("rows"), lax.axis_index("cols")
    last = count - 1
    inner = slice(HALO, HALO + side)
    body = slice(PAD, PAD + side)
    reach = side + 2 * FAR
    span = side + PAD

    load = pltpu.make_async_copy(x_ref, pads.at[0, inner, body], load_sem.at[0])
    load.start()

    def there(step):
        di, dj = step
        ok = []
        if di:
            ok.append(row > 0 if di < 0 else row < last)
        if dj:
            ok.append(col > 0 if dj < 0 else col < last)
        return ok[0] if len(ok) == 1 else jnp.logical_and(*ok)

    barrier = pltpu.get_barrier_semaphore()
    friends = (row != col).astype(jnp.int32)

    @pl.when(row != col)
    def _():
        pl.semaphore_signal(
            barrier, inc=1, device_id={"rows": col, "cols": row}, device_id_type=MESH
        )

    for step in SIDES:
        yes = there(step)
        friends += yes.astype(jnp.int32)

        @pl.when(yes)
        def _():
            pl.semaphore_signal(
                barrier, inc=1, device_id={"rows": row + step[0], "cols": col + step[1]},
                device_id_type=MESH,
            )

    load_near = pltpu.make_async_copy(near_ref, near, load_sem.at[1])
    load_far = pltpu.make_async_copy(far_ref, far, load_sem.at[2])
    load_near.start()
    load_far.start()

    def clear(ref):
        ref[...] = jnp.zeros(ref.shape, ref.dtype)

    def clear_off_map(ref, height, left, width):
        for at_edge, part in (
            (row == 0, (slice(0, height), slice(None))),
            (row == last, (slice(height + side, height * 2 + side), slice(None))),
            (col == 0, (slice(None), slice(left - width, left))),
            (col == last, (slice(None), slice(left + side, left + side + width))),
        ):
            pl.when(at_edge)(functools.partial(clear, ref.at[part]))

    def rim_copy(n, at):
        di, dj = SIDES[at]
        if di and dj:
            source, target = corners.at[n, 0, at], corners.at[n, 1, at]
        elif di:
            rows = slice(HALO, 2 * HALO) if di < 0 else slice(side, side + HALO)
            to = slice(HALO + side, 2 * HALO + side) if di < 0 else slice(0, HALO)
            source, target = pads.at[n, rows, body], pads.at[n, to, body]
        else:
            source = turned.at[n, 0 if dj < 0 else 1]
            target = strips.at[n, 1 if dj < 0 else 0]
        return pltpu.make_async_remote_copy(
            src_ref=source, dst_ref=target,
            send_sem=send_sem.at[n, at], recv_sem=recv_sem.at[n, at],
            device_id={"rows": row + di, "cols": col + dj}, device_id_type=MESH,
        )

    def rim_start(n, ats):
        for at in ats:
            @pl.when(there(SIDES[at]))
            def _():
                rim_copy(n, at).start()

    def rim(n, cells, head, tail):
        turned[n, 0] = head
        turned[n, 1] = tail
        rim_start(n, (0, 1))
        pads[n, inner, body] = cells
        for at in range(2, 6):
            di, dj = SIDES[at]
            rows = slice(0, HALO) if di < 0 else slice(side - HALO, side)
            bins = slice(0, PACK) if dj < 0 else slice(side - PACK, side)
            corners[n, 0, at] = cells[rows, bins].reshape(HALO * PACK, channels)
        rim_start(n, range(2, 8))

    def rim_wait(n):
        for at, (di, dj) in enumerate(SIDES):
            @pl.when(there((-di, -dj)))
            def _():
                rim_copy(n, at).wait_recv()
                if not di:
                    bins = slice(PAD - HALO, PAD) if dj > 0 else slice(
                        PAD + side, PAD + side + HALO)
                    pads[n, inner, bins] = flip(strips[n, 0 if dj > 0 else 1])
                elif dj:
                    rows = slice(0, HALO) if di > 0 else slice(HALO + side, 2 * HALO + side)
                    bins = slice(PAD - PACK, PAD) if dj > 0 else slice(
                        PAD + side, PAD + side + PACK)
                    pads[n, rows, bins] = corners[n, 1, at].reshape(HALO, PACK, channels)

    def hidden_of(n, weights):
        first, wide = PAD - HALO, weights.shape[1]
        shifted = [
            pads[n, :, first + NEAR * b:first + NEAR * b + span] for b in range(3)
        ]
        taps = [
            shifted[b][NEAR * a:NEAR * a + reach].reshape(reach * span, channels)
            for a in range(3) for b in range(3)
        ]
        total = jnp.dot(
            jnp.concatenate(taps, axis=1), weights, preferred_element_type=jnp.float32
        )
        hidden[..., :wide] = (
            jnp.maximum(total, 0.0).astype(hidden.dtype).reshape(reach, span, wide)
        )
        clear_off_map(hidden, FAR, FAR, FAR)

    def block_out_of(n, half, weights):
        lanes = slice(half * channels, (half + 1) * channels)
        shifted = [hidden[:, FAR * b:FAR * b + side, lanes] for b in range(3)]
        taps = [
            shifted[b][FAR * a:FAR * a + side].reshape(side * side, channels)
            for a in range(3) for b in range(3)
        ]
        total = jnp.dot(
            jnp.concatenate(taps, axis=1), weights, preferred_element_type=jnp.float32
        ).reshape(side, side, channels)
        return (pads[n, inner, body].astype(jnp.float32) + total).astype(jnp.bfloat16)

    def straight(w, n):
        return w[n].reshape(9 * channels, channels)

    def crossed(w, n):
        return jnp.concatenate([w[n, b, a] for a in range(3) for b in range(3)], axis=0)

    for n in range(blocks):
        clear_off_map(pads.at[n], HALO, PAD, PAD)

    load.wait()
    state = pads[0, inner, body]
    turn = flip(state)
    pl.semaphore_wait(barrier, friends)
    rim(0, state, turn[:HALO], turn[side - HALO:])
    load_near.wait()
    load_far.wait()

    for n in range(blocks):
        rim_wait(n)
        if n == 0:
            hidden_of(n, straight(near, n))
            block_out = block_out_of(n, 0, straight(far, n))
            mirror[0] = block_out
            swap = pltpu.make_async_remote_copy(
                src_ref=mirror.at[0], dst_ref=mirror.at[1],
                send_sem=mirror_sem.at[0], recv_sem=mirror_sem.at[1],
                device_id={"rows": col, "cols": row}, device_id_type=MESH,
            )

            @pl.when(row != col)
            def _():
                swap.start()

            @pl.when(row == col)
            def _():
                mirror[1] = block_out

            turn = flip(block_out)

            @pl.when(row != col)
            def _():
                swap.wait_recv()

            flipped = mirror[1]
            turn = average(turn, flipped)
            state = average(block_out, flip(flipped))
        else:
            hidden_of(n, jnp.concatenate([straight(near, n), crossed(near, n)], axis=1))
            block_out = block_out_of(n, 0, straight(far, n))
            state = average(block_out, block_out_of(n, 1, crossed(far, n)))
            turn = flip(state)
        if n < blocks - 1:
            rim(n + 1, state, turn[:HALO], turn[side - HALO:])
    out_ref[...] = state

    @pl.when(row != col)
    def _():
        swap.wait_send()

    for n in range(blocks):
        for at, step in enumerate(SIDES):
            @pl.when(there(step))
            def _():
                rim_copy(n, at).wait_send()


def by_tiles(contact_map, w_near, w_far):
    blocks, channels = w_near.shape[0], w_near.shape[-1]
    side, count = contact_map.shape[0], lax.axis_size("rows")
    kind = contact_map.dtype
    return pl.pallas_call(
        functools.partial(tile_kernel, count, side),
        out_shape=jax.ShapeDtypeStruct(contact_map.shape, kind),
        in_specs=[pl.BlockSpec(memory_space=pltpu.HBM)] * 3,
        out_specs=pl.BlockSpec(memory_space=pltpu.VMEM),
        scratch_shapes=[
            pltpu.VMEM((blocks, side + 2 * HALO, side + 2 * PAD, channels), kind),
            pltpu.VMEM((blocks, 2, HALO, side, channels), kind),
            pltpu.VMEM((blocks, 2, HALO, side, channels), kind),
            pltpu.VMEM((blocks, 2, len(SIDES), HALO * PACK, channels), kind),
            pltpu.VMEM((2, side, side, channels), kind),
            pltpu.VMEM((side + 2 * FAR, side + PAD, 2 * channels), kind),
            pltpu.VMEM(w_near.shape, kind),
            pltpu.VMEM(w_far.shape, kind),
            pltpu.SemaphoreType.DMA((3,)),
            pltpu.SemaphoreType.DMA((blocks, len(SIDES))),
            pltpu.SemaphoreType.DMA((blocks, len(SIDES))),
            pltpu.SemaphoreType.DMA((2,)),
        ],
        compiler_params=pltpu.CompilerParams(
            collective_id=0, has_side_effects=True, vmem_limit_bytes=64 * 2**20
        ),
    )(contact_map, w_near, w_far)


def on_device(contact_map, w_near, w_far):
    side = contact_map.shape[0]
    square = side == contact_map.shape[1] and side % PAD == 0
    if square and lax.axis_size("rows") == lax.axis_size("cols") and w_near.shape[0] > 1:
        return by_tiles(contact_map, w_near, w_far)
    return by_rows(contact_map, w_near, w_far)


def solution(mesh):
    in_specs = (P(("groups", "rows"), "cols", None), P(), P())
    out_specs = P(("groups", "rows"), "cols", None)
    return jax.shard_map(
        on_device, mesh=mesh, in_specs=in_specs, out_specs=out_specs, check_vma=False
    )
```

time: 23.6 us -> 21.5 us (0.911)
  local copies, waits for them, and re-layouts: 3.6 us -> 1.47 us
    unnamed x7 -> x1, local copies, waits for them, and re-layouts: 3.6 us -> 1.47 us
where the time goes in v2:
time: 21.5 us; the launch traced here: 21.3 us
  Pallas kernels  19.9 us (93%)
  local copies, waits for them, and re-layouts  1.47 us (7%)
    pallas_call x1, Pallas kernels, by_tiles(): pl.pallas_call(functools.partial(tile_kernel, count, side), out_shape=jax...  19.9 us
    unnamed x1, local copies, waits for them, and re-layouts  1.47 us

profile of v2, /device:TPU:1, one launch (start us, length us, event | category | flops | bytes accessed | tf_op | source)
XLA Modules:
  0.0 21.3 jit_solution(5303626806020163925)
XLA Ops:
  0.0 19.9 %shard_map.37 = bf16[16,16,128]{2,1,0:T(8,128)(2,1)} custom-call(bf16[16,16,128]{2,1,0:T(8,128)(2,1)} %x_ref.1, bf16[2,3,3,128,128]{4,3,2,1,0:T(8,128)(2,1)} %near_ref.1, bf16[2,3,3,128,128]{4,3,2,1,0:T(8,128)(2,1)} %far_ref.1), custom_call_target="tpu_custom_call" | custom-call | tf_op jit(solution)/shard_map/pallas_call | solution.py:287
  19.9 1.5 %copy.5 = bf16[16,16,128]{2,1,0:T(8,128)(2,1)} copy(bf16[16,16,128]{2,1,0:T(8,128)(2,1)} %shard_map.37) | data formatting | bytes 131072

commit v3 on v2

--- a/solution.py
+++ b/solution.py
@@ -11,7 +11,7 @@
 NEAR, FAR = 2, 4
 HALO = NEAR + FAR
 PAD, PACK = 16, 8
-SIDES = [(0, -1), (0, 1), (-1, -1), (-1, 1), (1, -1), (1, 1), (-1, 0), (1, 0)]
+SIDES = [(-1, 0), (1, 0), (0, -1), (0, 1), (-1, -1), (-1, 1), (1, -1), (1, 1)]
 
 
 def extended(cells, sides, width):
@@ -158,17 +158,18 @@
             def _():
                 rim_copy(n, at).start()
 
-    def rim(n, cells, head, tail):
-        turned[n, 0] = head
-        turned[n, 1] = tail
+    def send_columns(n, end, turn):
+        turned[n, end] = turn[:HALO] if end == 0 else turn[turn.shape[0] - HALO:]
+        rim_start(n, (2 + end,))
+
+    def send_rows(n, cells):
         rim_start(n, (0, 1))
-        pads[n, inner, body] = cells
-        for at in range(2, 6):
+        for at in range(4, 8):
             di, dj = SIDES[at]
             rows = slice(0, HALO) if di < 0 else slice(side - HALO, side)
             bins = slice(0, PACK) if dj < 0 else slice(side - PACK, side)
             corners[n, 0, at] = cells[rows, bins].reshape(HALO * PACK, channels)
-        rim_start(n, range(2, 8))
+        rim_start(n, range(4, 8))
 
     def rim_wait(n):
         for at, (di, dj) in enumerate(SIDES):
@@ -202,17 +203,21 @@
         )
         clear_off_map(hidden, FAR, FAR, FAR)
 
-    def block_out_of(n, half, weights):
+    def block_out_of(n, half, weights, rows):
         lanes = slice(half * channels, (half + 1) * channels)
-        shifted = [hidden[:, FAR * b:FAR * b + side, lanes] for b in range(3)]
+        start, size = rows.start, rows.stop - rows.start
+        shifted = [
+            hidden[start:rows.stop + 2 * FAR, FAR * b:FAR * b + side, lanes] for b in range(3)
+        ]
         taps = [
-            shifted[b][FAR * a:FAR * a + side].reshape(side * side, channels)
+            shifted[b][FAR * a:FAR * a + size].reshape(size * side, channels)
             for a in range(3) for b in range(3)
         ]
         total = jnp.dot(
             jnp.concatenate(taps, axis=1), weights, preferred_element_type=jnp.float32
-        ).reshape(side, side, channels)
-        return (pads[n, inner, body].astype(jnp.float32) + total).astype(jnp.bfloat16)
+        ).reshape(size, side, channels)
+        own = pads[n, HALO + start:HALO + rows.stop, body]
+        return (own.astype(jnp.float32) + total).astype(jnp.bfloat16)
 
     def straight(w, n):
         return w[n].reshape(9 * channels, channels)
@@ -223,11 +228,24 @@
     for n in range(blocks):
         clear_off_map(pads.at[n], HALO, PAD, PAD)
 
+    halves = [slice(0, side // 2), slice(side // 2, side)]
+    whole = slice(0, side)
+    swaps = [
+        pltpu.make_async_remote_copy(
+            src_ref=mirror.at[0, part], dst_ref=mirror.at[1, part],
+            send_sem=mirror_sem.at[0, k], recv_sem=mirror_sem.at[1, k],
+            device_id={"rows": col, "cols": row}, device_id_type=MESH,
+        )
+        for k, part in enumerate(halves)
+    ]
+
     load.wait()
+    pl.semaphore_wait(barrier, friends)
     state = pads[0, inner, body]
+    send_rows(0, state)
     turn = flip(state)
-    pl.semaphore_wait(barrier, friends)
-    rim(0, state, turn[:HALO], turn[side - HALO:])
+    send_columns(0, 0, turn)
+    send_columns(0, 1, turn)
     load_near.wait()
     load_far.wait()
 
@@ -235,43 +253,46 @@
         rim_wait(n)
         if n == 0:
             hidden_of(n, straight(near, n))
-            block_out = block_out_of(n, 0, straight(far, n))
-            mirror[0] = block_out
-            swap = pltpu.make_async_remote_copy(
-                src_ref=mirror.at[0], dst_ref=mirror.at[1],
-                send_sem=mirror_sem.at[0], recv_sem=mirror_sem.at[1],
-                device_id={"rows": col, "cols": row}, device_id_type=MESH,
-            )
-
-            @pl.when(row != col)
-            def _():
-                swap.start()
-
-            @pl.when(row == col)
-            def _():
-                mirror[1] = block_out
-
+            for swap, part in zip(swaps, halves):
+                mirror[0, part] = block_out_of(n, 0, straight(far, n), part)
+
+                @pl.when(row != col)
+                def _():
+                    swap.start()
+
+                @pl.when(row == col)
+                def _():
+                    mirror[1, part] = mirror[0, part]
+
+            block_out = mirror[0]
             turn = flip(block_out)
-
-            @pl.when(row != col)
-            def _():
-                swap.wait_recv()
-
-            flipped = mirror[1]
-            turn = average(turn, flipped)
-            state = average(block_out, flip(flipped))
+            for end, (swap, part) in enumerate(zip(swaps, halves)):
+                @pl.when(row != col)
+                def _():
+                    swap.wait_recv()
+
+                send_columns(n + 1, end, average(turn[part], mirror[1, part]))
+            state = average(block_out, flip(mirror[1]))
+            pads[n + 1, inner, body] = state
+            send_rows(n + 1, state)
         else:
             hidden_of(n, jnp.concatenate([straight(near, n), crossed(near, n)], axis=1))
-            block_out = block_out_of(n, 0, straight(far, n))
-            state = average(block_out, block_out_of(n, 1, crossed(far, n)))
-            turn = flip(state)
-        if n < blocks - 1:
-            rim(n + 1, state, turn[:HALO], turn[side - HALO:])
+            state = average(
+                block_out_of(n, 0, straight(far, n), whole),
+                block_out_of(n, 1, crossed(far, n), whole),
+            )
+            if n < blocks - 1:
+                pads[n + 1, inner, body] = state
+                send_rows(n + 1, state)
+                turn = flip(state)
+                send_columns(n + 1, 0, turn)
+                send_columns(n + 1, 1, turn)
     out_ref[...] = state
 
     @pl.when(row != col)
     def _():
-        swap.wait_send()
+        for swap in swaps:
+            swap.wait_send()
 
     for n in range(blocks):
         for at, step in enumerate(SIDES):
@@ -301,10 +322,10 @@
             pltpu.SemaphoreType.DMA((3,)),
             pltpu.SemaphoreType.DMA((blocks, len(SIDES))),
             pltpu.SemaphoreType.DMA((blocks, len(SIDES))),
-            pltpu.SemaphoreType.DMA((2,)),
+            pltpu.SemaphoreType.DMA((2, 2)),
         ],
         compiler_params=pltpu.CompilerParams(
-            collective_id=0, has_side_effects=True, vmem_limit_bytes=64 * 2**20
+            collective_id=0, has_side_effects=True, vmem_limit_bytes=107 * 2**19
         ),
     )(contact_map, w_near, w_far)
 

time: 21.5 us -> 20.6 us (0.958)
  Pallas kernels: 19.9 us -> 19 us
    pallas_call x1, Pallas kernels: 19.9 us -> 19 us  [by_tiles(): pl.pallas_call(functools.partial(tile_kernel, count, side), out_shape=jax...]
    unnamed x1 -> x3, local copies, waits for them, and re-layouts: 1.47 us -> 1.47 us
where the time goes in v3:
time: 20.6 us; the launch traced here: 20.5 us
  Pallas kernels  19 us (92%)
  local copies, waits for them, and re-layouts  1.47 us (7%)
    pallas_call x1, Pallas kernels, by_tiles(): pl.pallas_call(functools.partial(tile_kernel, count, side), out_shape=jax...  19 us
    unnamed x3, local copies, waits for them, and re-layouts  1.47 us

profile of v3, /device:TPU:1, one launch (start us, length us, event | category | flops | bytes accessed | tf_op | source)
XLA Modules:
  0.0 20.5 jit_solution(5658972135220776686)
XLA Ops:
  0.0 0.0 copy-start
  0.0 0.8 %copy-done = bf16[16,16,128]{2,1,0:T(8,128)(2,1)S(1)} copy-done((bf16[16,16,128]{2,1,0:T(8,128)(2,1)S(1)}, bf16[16,16,128]{2,1,0:T(8,128)(2,1)}, u32[]{:S(2)}) %copy-start) | copy-done | bytes 65560
  0.8 19.0 %shard_map.37 = bf16[16,16,128]{2,1,0:T(8,128)(2,1)S(1)} custom-call(bf16[16,16,128]{2,1,0:T(8,128)(2,1)S(1)} %copy-done, bf16[2,3,3,128,128]{4,3,2,1,0:T(8,128)(2,1)} %near_ref.1, bf16[2,3,3,128,128]{4,3,2,1,0:T(8,128)(2,1)} %far_ref.1), custom_call_target="tpu_custom_call" | custom-call | tf_op jit(solution)/shard_map/pallas_call | solution.py:308
  19.8 0.6 %copy.5 = bf16[16,16,128]{2,1,0:T(8,128)(2,1)} copy(bf16[16,16,128]{2,1,0:T(8,128)(2,1)S(1)} %shard_map.37) | data formatting | bytes 131072
Async XLA Ops:
  0.0 0.8 %copy-start = (bf16[16,16,128]{2,1,0:T(8,128)(2,1)S(1)}, bf16[16,16,128]{2,1,0:T(8,128)(2,1)}, u32[]{:S(2)}) copy-start(bf16[16,16,128]{2,1,0:T(8,128)(2,1)} %x_ref.1) | copy-start | bytes 196612

commit v4 on v3

--- a/solution.py
+++ b/solution.py
@@ -162,8 +162,10 @@
         turned[n, end] = turn[:HALO] if end == 0 else turn[turn.shape[0] - HALO:]
         rim_start(n, (2 + end,))
 
-    def send_rows(n, cells):
+    def send_rows(n):
         rim_start(n, (0, 1))
+
+    def send_corners(n, cells):
         for at in range(4, 8):
             di, dj = SIDES[at]
             rows = slice(0, HALO) if di < 0 else slice(side - HALO, side)
@@ -171,8 +173,11 @@
             corners[n, 0, at] = cells[rows, bins].reshape(HALO * PACK, channels)
         rim_start(n, range(4, 8))
 
-    def rim_wait(n):
+    def rim_wait(n, which):
         for at, (di, dj) in enumerate(SIDES):
+            if di != which:
+                continue
+
             @pl.when(there((-di, -dj)))
             def _():
                 rim_copy(n, at).wait_recv()
@@ -186,21 +191,32 @@
                         PAD + side, PAD + side + PACK)
                     pads[n, rows, bins] = corners[n, 1, at].reshape(HALO, PACK, channels)
 
-    def hidden_of(n, weights):
+    def hidden_rows(n, weights, start, size):
         first, wide = PAD - HALO, weights.shape[1]
         shifted = [
-            pads[n, :, first + NEAR * b:first + NEAR * b + span] for b in range(3)
+            pads[n, pl.ds(start, size + 2 * NEAR), first + NEAR * b:first + NEAR * b + span]
+            for b in range(3)
         ]
         taps = [
-            shifted[b][NEAR * a:NEAR * a + reach].reshape(reach * span, channels)
+            shifted[b][NEAR * a:NEAR * a + size].reshape(size * span, channels)
             for a in range(3) for b in range(3)
         ]
         total = jnp.dot(
             jnp.concatenate(taps, axis=1), weights, preferred_element_type=jnp.float32
         )
-        hidden[..., :wide] = (
-            jnp.maximum(total, 0.0).astype(hidden.dtype).reshape(reach, span, wide)
-        )
+        hidden[pl.ds(start, size), :, :wide] = (
+            jnp.maximum(total, 0.0).astype(hidden.dtype).reshape(size, span, wide)
+        )
+
+    def hidden_of(n, weights):
+        rim_wait(n, 0)
+        hidden_rows(n, weights, HALO, side - 2 * NEAR)
+        odd = lax.rem(row, 2)
+        for k in range(2):
+            above = odd == 1 - k
+            pl.when(above)(functools.partial(rim_wait, n, 1))
+            pl.when(jnp.logical_not(above))(functools.partial(rim_wait, n, -1))
+            hidden_rows(n, weights, jnp.where(above, 0, reach - HALO), HALO)
         clear_off_map(hidden, FAR, FAR, FAR)
 
     def block_out_of(n, half, weights, rows):
@@ -241,16 +257,16 @@
 
     load.wait()
     pl.semaphore_wait(barrier, friends)
+    send_rows(0)
     state = pads[0, inner, body]
-    send_rows(0, state)
     turn = flip(state)
     send_columns(0, 0, turn)
     send_columns(0, 1, turn)
+    send_corners(0, state)
     load_near.wait()
     load_far.wait()
 
     for n in range(blocks):
-        rim_wait(n)
         if n == 0:
             hidden_of(n, straight(near, n))
             for swap, part in zip(swaps, halves):
@@ -274,7 +290,8 @@
                 send_columns(n + 1, end, average(turn[part], mirror[1, part]))
             state = average(block_out, flip(mirror[1]))
             pads[n + 1, inner, body] = state
-            send_rows(n + 1, state)
+            send_rows(n + 1)
+            send_corners(n + 1, state)
         else:
             hidden_of(n, jnp.concatenate([straight(near, n), crossed(near, n)], axis=1))
             state = average(
@@ -283,10 +300,11 @@
             )
             if n < blocks - 1:
                 pads[n + 1, inner, body] = state
-                send_rows(n + 1, state)
                 turn = flip(state)
                 send_columns(n + 1, 0, turn)
                 send_columns(n + 1, 1, turn)
+                send_rows(n + 1)
+                send_corners(n + 1, state)
     out_ref[...] = state
 
     @pl.when(row != col)

time: 20.6 us -> 19.3 us (0.937)
  Pallas kernels: 19 us -> 17.7 us
    pallas_call x1, Pallas kernels: 19 us -> 17.7 us  [by_tiles(): pl.pallas_call(functools.partial(tile_kernel, count, side), out_shape=jax...]
where the time goes in v4:
time: 19.3 us; the launch traced here: 19.2 us
  Pallas kernels  17.7 us (92%)
  local copies, waits for them, and re-layouts  1.47 us (8%)
    pallas_call x1, Pallas kernels, by_tiles(): pl.pallas_call(functools.partial(tile_kernel, count, side), out_shape=jax...  17.7 us
    unnamed x3, local copies, waits for them, and re-layouts  1.47 us

profile of v4, /device:TPU:1, one launch (start us, length us, event | category | flops | bytes accessed | tf_op | source)
XLA Modules:
  0.0 19.2 jit_solution(11488139686456132202)
XLA Ops:
  0.0 0.0 copy-start
  0.0 0.8 %copy-done = bf16[16,16,128]{2,1,0:T(8,128)(2,1)S(1)} copy-done((bf16[16,16,128]{2,1,0:T(8,128)(2,1)S(1)}, bf16[16,16,128]{2,1,0:T(8,128)(2,1)}, u32[]{:S(2)}) %copy-start) | copy-done | bytes 65560
  0.8 17.7 %shard_map.37 = bf16[16,16,128]{2,1,0:T(8,128)(2,1)S(1)} custom-call(bf16[16,16,128]{2,1,0:T(8,128)(2,1)S(1)} %copy-done, bf16[2,3,3,128,128]{4,3,2,1,0:T(8,128)(2,1)} %near_ref.1, bf16[2,3,3,128,128]{4,3,2,1,0:T(8,128)(2,1)} %far_ref.1), custom_call_target="tpu_custom_call" | custom-call | tf_op jit(solution)/shard_map/pallas_call | solution.py:326
  18.6 0.6 %copy.5 = bf16[16,16,128]{2,1,0:T(8,128)(2,1)} copy(bf16[16,16,128]{2,1,0:T(8,128)(2,1)S(1)} %shard_map.37) | data formatting | bytes 131072
Async XLA Ops:
  0.0 0.8 %copy-start = (bf16[16,16,128]{2,1,0:T(8,128)(2,1)S(1)}, bf16[16,16,128]{2,1,0:T(8,128)(2,1)}, u32[]{:S(2)}) copy-start(bf16[16,16,128]{2,1,0:T(8,128)(2,1)} %x_ref.1) | copy-start | bytes 196612

commit v5 on v4

--- a/solution.py
+++ b/solution.py
@@ -85,6 +85,7 @@
     body = slice(PAD, PAD + side)
     reach = side + 2 * FAR
     span = side + PAD
+    half = side // 2
 
     load = pltpu.make_async_copy(x_ref, pads.at[0, inner, body], load_sem.at[0])
     load.start()
@@ -208,32 +209,32 @@
             jnp.maximum(total, 0.0).astype(hidden.dtype).reshape(size, span, wide)
         )
 
-    def hidden_of(n, weights):
-        rim_wait(n, 0)
-        hidden_rows(n, weights, HALO, side - 2 * NEAR)
-        odd = lax.rem(row, 2)
-        for k in range(2):
-            above = odd == 1 - k
-            pl.when(above)(functools.partial(rim_wait, n, 1))
-            pl.when(jnp.logical_not(above))(functools.partial(rim_wait, n, -1))
-            hidden_rows(n, weights, jnp.where(above, 0, reach - HALO), HALO)
-        clear_off_map(hidden, FAR, FAR, FAR)
-
-    def block_out_of(n, half, weights, rows):
-        lanes = slice(half * channels, (half + 1) * channels)
-        start, size = rows.start, rows.stop - rows.start
+    def block_out_of(n, lane, weights, start):
+        lanes = slice(lane * channels, (lane + 1) * channels)
         shifted = [
-            hidden[start:rows.stop + 2 * FAR, FAR * b:FAR * b + side, lanes] for b in range(3)
+            hidden[pl.ds(start, half + 2 * FAR), FAR * b:FAR * b + side, lanes]
+            for b in range(3)
         ]
         taps = [
-            shifted[b][FAR * a:FAR * a + size].reshape(size * side, channels)
+            shifted[b][FAR * a:FAR * a + half].reshape(half * side, channels)
             for a in range(3) for b in range(3)
         ]
         total = jnp.dot(
             jnp.concatenate(taps, axis=1), weights, preferred_element_type=jnp.float32
-        ).reshape(size, side, channels)
-        own = pads[n, HALO + start:HALO + rows.stop, body]
+        ).reshape(half, side, channels)
+        own = pads[n, pl.ds(HALO + start, half), body]
         return (own.astype(jnp.float32) + total).astype(jnp.bfloat16)
+
+    def halves_of(n, weights, half_done):
+        rim_wait(n, 0)
+        hidden_rows(n, weights, HALO, side - 2 * NEAR)
+        for k in range(2):
+            above = lax.rem(row, 2) == 1 - k
+            pl.when(above)(functools.partial(rim_wait, n, 1))
+            pl.when(jnp.logical_not(above))(functools.partial(rim_wait, n, -1))
+            hidden_rows(n, weights, jnp.where(above, 0, reach - HALO), HALO)
+            clear_off_map(hidden, FAR, FAR, FAR)
+            half_done(k, jnp.where(above, 0, half))
 
     def straight(w, n):
         return w[n].reshape(9 * channels, channels)
@@ -244,16 +245,44 @@
     for n in range(blocks):
         clear_off_map(pads.at[n], HALO, PAD, PAD)
 
-    halves = [slice(0, side // 2), slice(side // 2, side)]
-    whole = slice(0, side)
-    swaps = [
-        pltpu.make_async_remote_copy(
+    def swap(k, start):
+        part = pl.ds(start, half)
+        return pltpu.make_async_remote_copy(
             src_ref=mirror.at[0, part], dst_ref=mirror.at[1, part],
             send_sem=mirror_sem.at[0, k], recv_sem=mirror_sem.at[1, k],
             device_id={"rows": col, "cols": row}, device_id_type=MESH,
         )
-        for k, part in enumerate(halves)
-    ]
+
+    def mirror_half(k, start):
+        part = pl.ds(start, half)
+        mirror[0, part] = block_out_of(0, 0, straight(far, 0), start)
+
+        @pl.when(row != col)
+        def _():
+            swap(k, start).start()
+
+        @pl.when(row == col)
+        def _():
+            mirror[1, part] = mirror[0, part]
+
+    def columns_half(n, k, end, turn):
+        part = slice(end * half, (end + 1) * half)
+
+        @pl.when(row != col)
+        def _():
+            swap(k, end * half).wait_recv()
+
+        send_columns(n, end, average(turn[part], mirror[1, part]))
+
+    def average_half(n, k, start):
+        value = average(
+            block_out_of(n, 0, straight(far, n), start),
+            block_out_of(n, 1, crossed(far, n), start),
+        )
+        if n == blocks - 1:
+            out_ref[pl.ds(start, half)] = value
+        else:
+            pads[n + 1, pl.ds(HALO + start, half), body] = value
 
     load.wait()
     pl.semaphore_wait(barrier, friends)
@@ -268,49 +297,35 @@
 
     for n in range(blocks):
         if n == 0:
-            hidden_of(n, straight(near, n))
-            for swap, part in zip(swaps, halves):
-                mirror[0, part] = block_out_of(n, 0, straight(far, n), part)
-
-                @pl.when(row != col)
-                def _():
-                    swap.start()
-
-                @pl.when(row == col)
-                def _():
-                    mirror[1, part] = mirror[0, part]
-
+            halves_of(n, straight(near, n), mirror_half)
             block_out = mirror[0]
             turn = flip(block_out)
-            for end, (swap, part) in enumerate(zip(swaps, halves)):
-                @pl.when(row != col)
-                def _():
-                    swap.wait_recv()
-
-                send_columns(n + 1, end, average(turn[part], mirror[1, part]))
+            for k in range(2):
+                for end in range(2):
+                    pl.when(lax.rem(col, 2) == (1 - k if end == 0 else k))(
+                        functools.partial(columns_half, n + 1, k, end, turn)
+                    )
             state = average(block_out, flip(mirror[1]))
             pads[n + 1, inner, body] = state
             send_rows(n + 1)
             send_corners(n + 1, state)
         else:
-            hidden_of(n, jnp.concatenate([straight(near, n), crossed(near, n)], axis=1))
-            state = average(
-                block_out_of(n, 0, straight(far, n), whole),
-                block_out_of(n, 1, crossed(far, n), whole),
+            halves_of(
+                n, jnp.concatenate([straight(near, n), crossed(near, n)], axis=1),
+                functools.partial(average_half, n),
             )
             if n < blocks - 1:
-                pads[n + 1, inner, body] = state
+                state = pads[n + 1, inner, body]
                 turn = flip(state)
                 send_columns(n + 1, 0, turn)
                 send_columns(n + 1, 1, turn)
                 send_rows(n + 1)
                 send_corners(n + 1, state)
-    out_ref[...] = state
 
     @pl.when(row != col)
     def _():
-        for swap in swaps:
-            swap.wait_send()
+        for k in range(2):
+            swap(k, jnp.where(lax.rem(row, 2) == 1 - k, 0, half)).wait_send()
 
     for n in range(blocks):
         for at, step in enumerate(SIDES):
@@ -343,7 +358,7 @@
             pltpu.SemaphoreType.DMA((2, 2)),
         ],
         compiler_params=pltpu.CompilerParams(
-            collective_id=0, has_side_effects=True, vmem_limit_bytes=107 * 2**19
+            collective_id=0, has_side_effects=True, vmem_limit_bytes=431 * 2**17
         ),
     )(contact_map, w_near, w_far)
 

time: 19.3 us -> 18.4 us (0.953)
  local copies, waits for them, and re-layouts: 1.47 us -> 0.63 us
    unnamed x3 -> x1, local copies, waits for them, and re-layouts: 1.47 us -> 0.63 us
where the time goes in v5:
time: 18.4 us; the launch traced here: 18.2 us
  Pallas kernels  17.6 us (96%)
  local copies, waits for them, and re-layouts  0.63 us (3%)
    pallas_call x1, Pallas kernels, by_tiles(): pl.pallas_call(functools.partial(tile_kernel, count, side), out_shape=jax...  17.6 us
    unnamed x1, local copies, waits for them, and re-layouts  0.63 us

profile of v5, /device:TPU:1, one launch (start us, length us, event | category | flops | bytes accessed | tf_op | source)
XLA Modules:
  0.0 18.2 jit_solution(248512222448068686)
XLA Ops:
  0.0 17.6 %shard_map.37 = bf16[16,16,128]{2,1,0:T(8,128)(2,1)S(1)} custom-call(bf16[16,16,128]{2,1,0:T(8,128)(2,1)} %x_ref.1, bf16[2,3,3,128,128]{4,3,2,1,0:T(8,128)(2,1)} %near_ref.1, bf16[2,3,3,128,128]{4,3,2,1,0:T(8,128)(2,1)} %far_ref.1), custom_call_target="tpu_custom_call" | custom-call | tf_op jit(solution)/shard_map/pallas_call | solution.py:341
  17.6 0.6 %copy.5 = bf16[16,16,128]{2,1,0:T(8,128)(2,1)} copy(bf16[16,16,128]{2,1,0:T(8,128)(2,1)S(1)} %shard_map.37) | data formatting | bytes 131072

commit v6 on v5

--- a/solution.py
+++ b/solution.py
@@ -159,20 +159,21 @@
             def _():
                 rim_copy(n, at).start()
 
-    def send_columns(n, end, turn):
+    def pack_columns(n, end, turn):
         turned[n, end] = turn[:HALO] if end == 0 else turn[turn.shape[0] - HALO:]
-        rim_start(n, (2 + end,))
-
-    def send_rows(n):
-        rim_start(n, (0, 1))
-
-    def send_corners(n, cells):
+
+    def pack_corners(n, cells):
         for at in range(4, 8):
             di, dj = SIDES[at]
             rows = slice(0, HALO) if di < 0 else slice(side - HALO, side)
             bins = slice(0, PACK) if dj < 0 else slice(side - PACK, side)
             corners[n, 0, at] = cells[rows, bins].reshape(HALO * PACK, channels)
-        rim_start(n, range(4, 8))
+
+    def rim_sent(n):
+        for at, step in enumerate(SIDES):
+            @pl.when(there(step))
+            def _():
+                rim_copy(n, at).wait_send()
 
     def rim_wait(n, which):
         for at, (di, dj) in enumerate(SIDES):
@@ -225,7 +226,7 @@
         own = pads[n, pl.ds(HALO + start, half), body]
         return (own.astype(jnp.float32) + total).astype(jnp.bfloat16)
 
-    def halves_of(n, weights, half_done):
+    def halves_of(n, weights, half_done, between):
         rim_wait(n, 0)
         hidden_rows(n, weights, HALO, side - 2 * NEAR)
         for k in range(2):
@@ -235,6 +236,8 @@
             hidden_rows(n, weights, jnp.where(above, 0, reach - HALO), HALO)
             clear_off_map(hidden, FAR, FAR, FAR)
             half_done(k, jnp.where(above, 0, half))
+            if k == 0:
+                between()
 
     def straight(w, n):
         return w[n].reshape(9 * channels, channels)
@@ -272,7 +275,8 @@
         def _():
             swap(k, end * half).wait_recv()
 
-        send_columns(n, end, average(turn[part], mirror[1, part]))
+        pack_columns(n, end, average(turn[part], mirror[1, part]))
+        rim_start(n, (2 + end,))
 
     def average_half(n, k, start):
         value = average(
@@ -284,22 +288,29 @@
         else:
             pads[n + 1, pl.ds(HALO + start, half), body] = value
 
+    def mirror_sent():
+        @pl.when(row != col)
+        def _():
+            for k in range(2):
+                swap(k, jnp.where(lax.rem(row, 2) == 1 - k, 0, half)).wait_send()
+
     load.wait()
-    pl.semaphore_wait(barrier, friends)
-    send_rows(0)
     state = pads[0, inner, body]
     turn = flip(state)
-    send_columns(0, 0, turn)
-    send_columns(0, 1, turn)
-    send_corners(0, state)
+    pack_columns(0, 0, turn)
+    pack_columns(0, 1, turn)
+    pack_corners(0, state)
+    pl.semaphore_wait(barrier, friends)
+    rim_start(0, (2, 3, 0, 1, 4, 5, 6, 7))
     load_near.wait()
     load_far.wait()
 
     for n in range(blocks):
         if n == 0:
-            halves_of(n, straight(near, n), mirror_half)
+            halves_of(n, straight(near, n), mirror_half, lambda: None)
             block_out = mirror[0]
             turn = flip(block_out)
+            rim_sent(n)
             for k in range(2):
                 for end in range(2):
                     pl.when(lax.rem(col, 2) == (1 - k if end == 0 else k))(
@@ -307,31 +318,22 @@
                     )
             state = average(block_out, flip(mirror[1]))
             pads[n + 1, inner, body] = state
-            send_rows(n + 1)
-            send_corners(n + 1, state)
+            rim_start(n + 1, (0, 1))
+            pack_corners(n + 1, state)
+            rim_start(n + 1, (4, 5, 6, 7))
+            mirror_sent()
         else:
             halves_of(
                 n, jnp.concatenate([straight(near, n), crossed(near, n)], axis=1),
-                functools.partial(average_half, n),
+                functools.partial(average_half, n), functools.partial(rim_sent, n),
             )
             if n < blocks - 1:
                 state = pads[n + 1, inner, body]
                 turn = flip(state)
-                send_columns(n + 1, 0, turn)
-                send_columns(n + 1, 1, turn)
-                send_rows(n + 1)
-                send_corners(n + 1, state)
-
-    @pl.when(row != col)
-    def _():
-        for k in range(2):
-            swap(k, jnp.where(lax.rem(row, 2) == 1 - k, 0, half)).wait_send()
-
-    for n in range(blocks):
-        for at, step in enumerate(SIDES):
-            @pl.when(there(step))
-            def _():
-                rim_copy(n, at).wait_send()
+                pack_columns(n + 1, 0, turn)
+                pack_columns(n + 1, 1, turn)
+                pack_corners(n + 1, state)
+                rim_start(n + 1, (2, 3, 0, 1, 4, 5, 6, 7))
 
 
 def by_tiles(contact_map, w_near, w_far):

time: 18.4 us -> 18.3 us (level)
  no operation moved by 1% of the time
where the time goes in v6:
time: 18.3 us; the launch traced here: 18.2 us
  Pallas kernels  17.6 us (96%)
  local copies, waits for them, and re-layouts  0.63 us (3%)
    pallas_call x1, Pallas kernels, by_tiles(): pl.pallas_call(functools.partial(tile_kernel, count, side), out_shape=jax...  17.6 us
    unnamed x1, local copies, waits for them, and re-layouts  0.63 us

profile of v6, /device:TPU:1, one launch (start us, length us, event | category | flops | bytes accessed | tf_op | source)
XLA Modules:
  0.0 18.2 jit_solution(12549713753133376717)
XLA Ops:
  0.0 17.6 %shard_map.37 = bf16[16,16,128]{2,1,0:T(8,128)(2,1)S(1)} custom-call(bf16[16,16,128]{2,1,0:T(8,128)(2,1)} %x_ref.1, bf16[2,3,3,128,128]{4,3,2,1,0:T(8,128)(2,1)} %near_ref.1, bf16[2,3,3,128,128]{4,3,2,1,0:T(8,128)(2,1)} %far_ref.1), custom_call_target="tpu_custom_call" | custom-call | tf_op jit(solution)/shard_map/pallas_call | solution.py:343
  17.6 0.6 %copy.5 = bf16[16,16,128]{2,1,0:T(8,128)(2,1)} copy(bf16[16,16,128]{2,1,0:T(8,128)(2,1)S(1)} %shard_map.37) | data formatting | bytes 131072

commit v7 on v6

--- a/solution.py
+++ b/solution.py
@@ -226,18 +226,18 @@
         own = pads[n, pl.ds(HALO + start, half), body]
         return (own.astype(jnp.float32) + total).astype(jnp.bfloat16)
 
-    def halves_of(n, weights, half_done, between):
+    def halves_of(n, weights, half_done):
         rim_wait(n, 0)
         hidden_rows(n, weights, HALO, side - 2 * NEAR)
-        for k in range(2):
+
+        @pl.loop(0, 2)
+        def _(k):
             above = lax.rem(row, 2) == 1 - k
             pl.when(above)(functools.partial(rim_wait, n, 1))
             pl.when(jnp.logical_not(above))(functools.partial(rim_wait, n, -1))
             hidden_rows(n, weights, jnp.where(above, 0, reach - HALO), HALO)
             clear_off_map(hidden, FAR, FAR, FAR)
             half_done(k, jnp.where(above, 0, half))
-            if k == 0:
-                between()
 
     def straight(w, n):
         return w[n].reshape(9 * channels, channels)
@@ -307,7 +307,7 @@
 
     for n in range(blocks):
         if n == 0:
-            halves_of(n, straight(near, n), mirror_half, lambda: None)
+            halves_of(n, straight(near, n), mirror_half)
             block_out = mirror[0]
             turn = flip(block_out)
             rim_sent(n)
@@ -325,8 +325,9 @@
         else:
             halves_of(
                 n, jnp.concatenate([straight(near, n), crossed(near, n)], axis=1),
-                functools.partial(average_half, n), functools.partial(rim_sent, n),
+                functools.partial(average_half, n),
             )
+            rim_sent(n)
             if n < blocks - 1:
                 state = pads[n + 1, inner, body]
                 turn = flip(state)

time: 18.3 us -> 18.1 us (0.989)
  Pallas kernels: 17.6 us -> 17.3 us
    pallas_call x1, Pallas kernels: 17.6 us -> 17.3 us  [by_tiles(): pl.pallas_call(functools.partial(tile_kernel, count, side), out_shape=jax...]
where the time goes in v7:
time: 18.1 us; the launch traced here: 18 us
  Pallas kernels  17.3 us (96%)
  local copies, waits for them, and re-layouts  0.63 us (3%)
    pallas_call x1, Pallas kernels, by_tiles(): pl.pallas_call(functools.partial(tile_kernel, count, side), out_shape=jax...  17.3 us
    unnamed x1, local copies, waits for them, and re-layouts  0.63 us

profile of v7, /device:TPU:1, one launch (start us, length us, event | category | flops | bytes accessed | tf_op | source)
XLA Modules:
  0.0 18.0 jit_solution(575760313045509123)
XLA Ops:
  0.0 17.3 %shard_map.37 = bf16[16,16,128]{2,1,0:T(8,128)(2,1)S(1)} custom-call(bf16[16,16,128]{2,1,0:T(8,128)(2,1)} %x_ref.1, bf16[2,3,3,128,128]{4,3,2,1,0:T(8,128)(2,1)} %near_ref.1, bf16[2,3,3,128,128]{4,3,2,1,0:T(8,128)(2,1)} %far_ref.1), custom_call_target="tpu_custom_call" | custom-call | tf_op jit(solution)/shard_map/pallas_call | solution.py:344
  17.3 0.6 %copy.5 = bf16[16,16,128]{2,1,0:T(8,128)(2,1)} copy(bf16[16,16,128]{2,1,0:T(8,128)(2,1)S(1)} %shard_map.37) | data formatting | bytes 131072

commit v8 on v7

--- a/solution.py
+++ b/solution.py
@@ -145,7 +145,7 @@
             to = slice(HALO + side, 2 * HALO + side) if di < 0 else slice(0, HALO)
             source, target = pads.at[n, rows, body], pads.at[n, to, body]
         else:
-            source = turned.at[n, 0 if dj < 0 else 1]
+            source = turned.at[n, slice(0, HALO) if dj < 0 else slice(side - HALO, side)]
             target = strips.at[n, 1 if dj < 0 else 0]
         return pltpu.make_async_remote_copy(
             src_ref=source, dst_ref=target,
@@ -158,9 +158,6 @@
             @pl.when(there(SIDES[at]))
             def _():
                 rim_copy(n, at).start()
-
-    def pack_columns(n, end, turn):
-        turned[n, end] = turn[:HALO] if end == 0 else turn[turn.shape[0] - HALO:]
 
     def pack_corners(n, cells):
         for at in range(4, 8):
@@ -175,20 +172,37 @@
             def _():
                 rim_copy(n, at).wait_send()
 
-    def rim_wait(n, which):
-        for at, (di, dj) in enumerate(SIDES):
-            if di != which:
-                continue
-
-            @pl.when(there((-di, -dj)))
+    def wait_columns(n):
+        for at in (2, 3):
+            dj = SIDES[at][1]
+
+            @pl.when(there((0, -dj)))
             def _():
                 rim_copy(n, at).wait_recv()
-                if not di:
-                    bins = slice(PAD - HALO, PAD) if dj > 0 else slice(
-                        PAD + side, PAD + side + HALO)
-                    pads[n, inner, bins] = flip(strips[n, 0 if dj > 0 else 1])
-                elif dj:
-                    rows = slice(0, HALO) if di > 0 else slice(HALO + side, 2 * HALO + side)
+                bins = slice(PAD - HALO, PAD) if dj > 0 else slice(
+                    PAD + side, PAD + side + HALO)
+                pads[n, inner, bins] = flip(strips[n, 0 if dj > 0 else 1])
+
+    def wait_rows(n, above):
+        down = above.astype(jnp.int32)
+        rows = pl.ds(jnp.where(above, 0, HALO + side), HALO)
+
+        def landed(ref, at):
+            pltpu.make_async_remote_copy(
+                src_ref=ref, dst_ref=ref,
+                send_sem=send_sem.at[n, at], recv_sem=recv_sem.at[n, at],
+                device_id={"rows": row, "cols": col}, device_id_type=MESH,
+            ).wait_recv()
+
+        @pl.when(jnp.where(above, row, last - row) > 0)
+        def _():
+            landed(pads.at[n, rows, body], down)
+            for right, dj in enumerate((-1, 1)):
+                at = 4 + 2 * down + right
+
+                @pl.when(col < last if dj < 0 else col > 0)
+                def _():
+                    landed(corners.at[n, 1, at], at)
                     bins = slice(PAD - PACK, PAD) if dj > 0 else slice(
                         PAD + side, PAD + side + PACK)
                     pads[n, rows, bins] = corners[n, 1, at].reshape(HALO, PACK, channels)
@@ -227,17 +241,26 @@
         return (own.astype(jnp.float32) + total).astype(jnp.bfloat16)
 
     def halves_of(n, weights, half_done):
-        rim_wait(n, 0)
-        hidden_rows(n, weights, HALO, side - 2 * NEAR)
-
-        @pl.loop(0, 2)
-        def _(k):
+        wait_columns(n)
+        middle = -(-(side - 2 * NEAR) // HALO)
+
+        @pl.loop(0, middle + 2)
+        def _(step):
+            k = step - middle
             above = lax.rem(row, 2) == 1 - k
-            pl.when(above)(functools.partial(rim_wait, n, 1))
-            pl.when(jnp.logical_not(above))(functools.partial(rim_wait, n, -1))
-            hidden_rows(n, weights, jnp.where(above, 0, reach - HALO), HALO)
-            clear_off_map(hidden, FAR, FAR, FAR)
-            half_done(k, jnp.where(above, 0, half))
+
+            @pl.when(k >= 0)
+            def _():
+                wait_rows(n, above)
+
+            between = jnp.minimum(HALO * (step + 1), reach - 2 * HALO)
+            ends = jnp.where(above, 0, reach - HALO)
+            hidden_rows(n, weights(), jnp.where(k < 0, between, ends), HALO)
+
+            @pl.when(k >= 0)
+            def _():
+                clear_off_map(hidden, FAR, FAR, FAR)
+                half_done(k, jnp.where(above, 0, half))
 
     def straight(w, n):
         return w[n].reshape(9 * channels, channels)
@@ -268,15 +291,17 @@
         def _():
             mirror[1, part] = mirror[0, part]
 
-    def columns_half(n, k, end, turn):
-        part = slice(end * half, (end + 1) * half)
+    def columns_half(n, k):
+        end = jnp.where(lax.rem(col, 2) == 1 - k, 0, 1)
+        part = pl.ds(end * half, half)
 
         @pl.when(row != col)
         def _():
             swap(k, end * half).wait_recv()
 
-        pack_columns(n, end, average(turn[part], mirror[1, part]))
-        rim_start(n, (2 + end,))
+        turned[n, part] = average(turned[n, part], mirror[1, part])
+        for at in (2, 3):
+            pl.when(end == at - 2)(functools.partial(rim_start, n, (at,)))
 
     def average_half(n, k, start):
         value = average(
@@ -296,9 +321,7 @@
 
     load.wait()
     state = pads[0, inner, body]
-    turn = flip(state)
-    pack_columns(0, 0, turn)
-    pack_columns(0, 1, turn)
+    turned[0] = flip(state)
     pack_corners(0, state)
     pl.semaphore_wait(barrier, friends)
     rim_start(0, (2, 3, 0, 1, 4, 5, 6, 7))
@@ -307,16 +330,11 @@
 
     for n in range(blocks):
         if n == 0:
-            halves_of(n, straight(near, n), mirror_half)
-            block_out = mirror[0]
-            turn = flip(block_out)
+            halves_of(n, lambda: straight(near, n), mirror_half)
+            turned[n + 1] = flip(mirror[0])
             rim_sent(n)
-            for k in range(2):
-                for end in range(2):
-                    pl.when(lax.rem(col, 2) == (1 - k if end == 0 else k))(
-                        functools.partial(columns_half, n + 1, k, end, turn)
-                    )
-            state = average(block_out, flip(mirror[1]))
+            pl.loop(0, 2)(functools.partial(columns_half, n + 1))
+            state = flip(turned[n + 1])
             pads[n + 1, inner, body] = state
             rim_start(n + 1, (0, 1))
             pack_corners(n + 1, state)
@@ -324,15 +342,13 @@
             mirror_sent()
         else:
             halves_of(
-                n, jnp.concatenate([straight(near, n), crossed(near, n)], axis=1),
+                n, lambda: jnp.concatenate([straight(near, n), crossed(near, n)], axis=1),
                 functools.partial(average_half, n),
             )
             rim_sent(n)
             if n < blocks - 1:
                 state = pads[n + 1, inner, body]
-                turn = flip(state)
-                pack_columns(n + 1, 0, turn)
-                pack_columns(n + 1, 1, turn)
+                turned[n + 1] = flip(state)
                 pack_corners(n + 1, state)
                 rim_start(n + 1, (2, 3, 0, 1, 4, 5, 6, 7))
 
@@ -348,7 +364,7 @@
         out_specs=pl.BlockSpec(memory_space=pltpu.VMEM),
         scratch_shapes=[
             pltpu.VMEM((blocks, side + 2 * HALO, side + 2 * PAD, channels), kind),
-            pltpu.VMEM((blocks, 2, HALO, side, channels), kind),
+            pltpu.VMEM((blocks, side, side, channels), kind),
             pltpu.VMEM((blocks, 2, HALO, side, channels), kind),
             pltpu.VMEM((blocks, 2, len(SIDES), HALO * PACK, channels), kind),
             pltpu.VMEM((2, side, side, channels), kind),

time: 18.1 us -> 18 us (level)
  no operation moved by 1% of the time
where the time goes in v8:
time: 18 us; the launch traced here: 17.9 us
  Pallas kernels  17.2 us (96%)
  local copies, waits for them, and re-layouts  0.63 us (4%)
    pallas_call x1, Pallas kernels, by_tiles(): pl.pallas_call(functools.partial(tile_kernel, count, side), out_shape=jax...  17.2 us
    unnamed x1, local copies, waits for them, and re-layouts  0.63 us

profile of v8, /device:TPU:1, one launch (start us, length us, event | category | flops | bytes accessed | tf_op | source)
XLA Modules:
  0.0 17.9 jit_solution(1145761122676344712)
XLA Ops:
  0.0 17.2 %shard_map.37 = bf16[16,16,128]{2,1,0:T(8,128)(2,1)S(1)} custom-call(bf16[16,16,128]{2,1,0:T(8,128)(2,1)} %x_ref.1, bf16[2,3,3,128,128]{4,3,2,1,0:T(8,128)(2,1)} %near_ref.1, bf16[2,3,3,128,128]{4,3,2,1,0:T(8,128)(2,1)} %far_ref.1), custom_call_target="tpu_custom_call" | custom-call | tf_op jit(solution)/shard_map/pallas_call | solution.py:360
  17.2 0.6 %copy.5 = bf16[16,16,128]{2,1,0:T(8,128)(2,1)} copy(bf16[16,16,128]{2,1,0:T(8,128)(2,1)S(1)} %shard_map.37) | data formatting | bytes 131072

commit v9 on v8

--- a/solution.py
+++ b/solution.py
@@ -119,10 +119,11 @@
                 device_id_type=MESH,
             )
 
-    load_near = pltpu.make_async_copy(near_ref, near, load_sem.at[1])
-    load_far = pltpu.make_async_copy(far_ref, far, load_sem.at[2])
-    load_near.start()
-    load_far.start()
+    def weight_loads(n):
+        return (
+            pltpu.make_async_copy(near_ref.at[n], near.at[n], load_sem.at[1 + 2 * n]),
+            pltpu.make_async_copy(far_ref.at[n], far.at[n], load_sem.at[2 + 2 * n]),
+        )
 
     def clear(ref):
         ref[...] = jnp.zeros(ref.shape, ref.dtype)
@@ -242,6 +243,8 @@
 
     def halves_of(n, weights, half_done):
         wait_columns(n)
+        for copy in weight_loads(n):
+            copy.wait()
         middle = -(-(side - 2 * NEAR) // HALO)
 
         @pl.loop(0, middle + 2)
@@ -320,17 +323,19 @@
                 swap(k, jnp.where(lax.rem(row, 2) == 1 - k, 0, half)).wait_send()
 
     load.wait()
+    for copy in weight_loads(0):
+        copy.start()
     state = pads[0, inner, body]
     turned[0] = flip(state)
     pack_corners(0, state)
     pl.semaphore_wait(barrier, friends)
     rim_start(0, (2, 3, 0, 1, 4, 5, 6, 7))
-    load_near.wait()
-    load_far.wait()
 
     for n in range(blocks):
         if n == 0:
             halves_of(n, lambda: straight(near, n), mirror_half)
+            for copy in weight_loads(n + 1):
+                copy.start()
             turned[n + 1] = flip(mirror[0])
             rim_sent(n)
             pl.loop(0, 2)(functools.partial(columns_half, n + 1))
@@ -347,6 +352,8 @@
             )
             rim_sent(n)
             if n < blocks - 1:
+                for copy in weight_loads(n + 1):
+                    copy.start()
                 state = pads[n + 1, inner, body]
                 turned[n + 1] = flip(state)
                 pack_corners(n + 1, state)
@@ -371,7 +378,7 @@
             pltpu.VMEM((side + 2 * FAR, side + PAD, 2 * channels), kind),
             pltpu.VMEM(w_near.shape, kind),
             pltpu.VMEM(w_far.shape, kind),
-            pltpu.SemaphoreType.DMA((3,)),
+            pltpu.SemaphoreType.DMA((1 + 2 * blocks,)),
             pltpu.SemaphoreType.DMA((blocks, len(SIDES))),
             pltpu.SemaphoreType.DMA((blocks, len(SIDES))),
             pltpu.SemaphoreType.DMA((2, 2)),

time: 18 us -> 18 us (level)
  no operation moved by 1% of the time
where the time goes in v9:
time: 18 us; the launch traced here: 17.9 us
  Pallas kernels  17.3 us (96%)
  local copies, waits for them, and re-layouts  0.63 us (4%)
    pallas_call x1, Pallas kernels, by_tiles(): pl.pallas_call(functools.partial(tile_kernel, count, side), out_shape=jax...  17.3 us
    unnamed x1, local copies, waits for them, and re-layouts  0.63 us

profile of v9, /device:TPU:1, one launch (start us, length us, event | category | flops | bytes accessed | tf_op | source)
XLA Modules:
  0.0 17.9 jit_solution(9900589027047425779)
XLA Ops:
  0.0 17.3 %shard_map.37 = bf16[16,16,128]{2,1,0:T(8,128)(2,1)S(1)} custom-call(bf16[16,16,128]{2,1,0:T(8,128)(2,1)} %x_ref.1, bf16[2,3,3,128,128]{4,3,2,1,0:T(8,128)(2,1)} %near_ref.1, bf16[2,3,3,128,128]{4,3,2,1,0:T(8,128)(2,1)} %far_ref.1), custom_call_target="tpu_custom_call" | custom-call | tf_op jit(solution)/shard_map/pallas_call | solution.py:367
  17.3 0.6 %copy.5 = bf16[16,16,128]{2,1,0:T(8,128)(2,1)} copy(bf16[16,16,128]{2,1,0:T(8,128)(2,1)S(1)} %shard_map.37) | data formatting | bytes 131072

commit v10 on v9

--- a/solution.py
+++ b/solution.py
@@ -160,12 +160,11 @@
             def _():
                 rim_copy(n, at).start()
 
-    def pack_corners(n, cells):
-        for at in range(4, 8):
-            di, dj = SIDES[at]
-            rows = slice(0, HALO) if di < 0 else slice(side - HALO, side)
-            bins = slice(0, PACK) if dj < 0 else slice(side - PACK, side)
-            corners[n, 0, at] = cells[rows, bins].reshape(HALO * PACK, channels)
+    def pack_corners(n, end):
+        bins = slice(0, HALO) if end == 0 else slice(side - HALO, side)
+        for at in (4 + end, 6 + end):
+            rows = slice(0, PACK) if SIDES[at][0] < 0 else slice(side - PACK, side)
+            corners[n, 0, at] = turned[n, bins, rows].reshape(HALO * PACK, channels)
 
     def rim_sent(n):
         for at, step in enumerate(SIDES):
@@ -204,9 +203,11 @@
                 @pl.when(col < last if dj < 0 else col > 0)
                 def _():
                     landed(corners.at[n, 1, at], at)
-                    bins = slice(PAD - PACK, PAD) if dj > 0 else slice(
-                        PAD + side, PAD + side + PACK)
-                    pads[n, rows, bins] = corners[n, 1, at].reshape(HALO, PACK, channels)
+                    bins = slice(PAD - HALO, PAD) if dj > 0 else slice(
+                        PAD + side, PAD + side + HALO)
+                    corner = flip(corners[n, 1, at].reshape(HALO, PACK, channels))
+                    pads[n, rows, bins] = jnp.where(
+                        above, corner[PACK - HALO:], corner[:HALO])
 
     def hidden_rows(n, weights, start, size):
         first, wide = PAD - HALO, weights.shape[1]
@@ -303,8 +304,12 @@
             swap(k, end * half).wait_recv()
 
         turned[n, part] = average(turned[n, part], mirror[1, part])
-        for at in (2, 3):
-            pl.when(end == at - 2)(functools.partial(rim_start, n, (at,)))
+        for which in range(2):
+            @pl.when(end == which)
+            def _():
+                rim_start(n, (2 + which,))
+                pack_corners(n, which)
+                rim_start(n, (4 + which, 6 + which))
 
     def average_half(n, k, start):
         value = average(
@@ -327,7 +332,8 @@
         copy.start()
     state = pads[0, inner, body]
     turned[0] = flip(state)
-    pack_corners(0, state)
+    pack_corners(0, 0)
+    pack_corners(0, 1)
     pl.semaphore_wait(barrier, friends)
     rim_start(0, (2, 3, 0, 1, 4, 5, 6, 7))
 
@@ -342,8 +348,6 @@
             state = flip(turned[n + 1])
             pads[n + 1, inner, body] = state
             rim_start(n + 1, (0, 1))
-            pack_corners(n + 1, state)
-            rim_start(n + 1, (4, 5, 6, 7))
             mirror_sent()
         else:
             halves_of(
@@ -356,7 +360,8 @@
                     copy.start()
                 state = pads[n + 1, inner, body]
                 turned[n + 1] = flip(state)
-                pack_corners(n + 1, state)
+                pack_corners(n + 1, 0)
+                pack_corners(n + 1, 1)
                 rim_start(n + 1, (2, 3, 0, 1, 4, 5, 6, 7))
 
 

time: 18 us -> 18.1 us (level)
  no operation moved by 1% of the time
where the time goes in v10:
time: 18.1 us; the launch traced here: 17.9 us
  Pallas kernels  17.3 us (96%)
  local copies, waits for them, and re-layouts  0.63 us (3%)
    pallas_call x1, Pallas kernels, by_tiles(): pl.pallas_call(functools.partial(tile_kernel, count, side), out_shape=jax...  17.3 us
    unnamed x1, local copies, waits for them, and re-layouts  0.63 us

profile of v10, /device:TPU:1, one launch (start us, length us, event | category | flops | bytes accessed | tf_op | source)
XLA Modules:
  0.0 17.9 jit_solution(10617259089594388642)
XLA Ops:
  0.0 17.3 %shard_map.37 = bf16[16,16,128]{2,1,0:T(8,128)(2,1)S(1)} custom-call(bf16[16,16,128]{2,1,0:T(8,128)(2,1)} %x_ref.1, bf16[2,3,3,128,128]{4,3,2,1,0:T(8,128)(2,1)} %near_ref.1, bf16[2,3,3,128,128]{4,3,2,1,0:T(8,128)(2,1)} %far_ref.1), custom_call_target="tpu_custom_call" | custom-call | tf_op jit(solution)/shard_map/pallas_call | solution.py:372
  17.3 0.6 %copy.5 = bf16[16,16,128]{2,1,0:T(8,128)(2,1)} copy(bf16[16,16,128]{2,1,0:T(8,128)(2,1)S(1)} %shard_map.37) | data formatting | bytes 131072

commit v11 on v10

--- a/solution.py
+++ b/solution.py
@@ -295,15 +295,19 @@
         def _():
             mirror[1, part] = mirror[0, part]
 
+    def end_of(k):
+        return jnp.where(lax.rem(col, 2) == 1 - k, 0, 1)
+
     def columns_half(n, k):
-        end = jnp.where(lax.rem(col, 2) == 1 - k, 0, 1)
-        part = pl.ds(end * half, half)
+        part = pl.ds(end_of(k) * half, half)
 
         @pl.when(row != col)
         def _():
-            swap(k, end * half).wait_recv()
+            swap(k, end_of(k) * half).wait_recv()
 
         turned[n, part] = average(turned[n, part], mirror[1, part])
+
+    def send_end(n, end):
         for which in range(2):
             @pl.when(end == which)
             def _():
@@ -344,10 +348,13 @@
                 copy.start()
             turned[n + 1] = flip(mirror[0])
             rim_sent(n)
-            pl.loop(0, 2)(functools.partial(columns_half, n + 1))
+            columns_half(n + 1, 0)
+            send_end(n + 1, end_of(0))
+            columns_half(n + 1, 1)
             state = flip(turned[n + 1])
             pads[n + 1, inner, body] = state
             rim_start(n + 1, (0, 1))
+            send_end(n + 1, end_of(1))
             mirror_sent()
         else:
             halves_of(

time: 18.1 us -> 18 us (level)
  no operation moved by 1% of the time
where the time goes in v11:
time: 18 us; the launch traced here: 17.9 us
  Pallas kernels  17.3 us (96%)
  local copies, waits for them, and re-layouts  0.63 us (4%)
    pallas_call x1, Pallas kernels, by_tiles(): pl.pallas_call(functools.partial(tile_kernel, count, side), out_shape=jax...  17.3 us
    unnamed x1, local copies, waits for them, and re-layouts  0.63 us

profile of v11, /device:TPU:1, one launch (start us, length us, event | category | flops | bytes accessed | tf_op | source)
XLA Modules:
  0.0 17.9 jit_solution(41517517910812999)
XLA Ops:
  0.0 17.3 %shard_map.37 = bf16[16,16,128]{2,1,0:T(8,128)(2,1)S(1)} custom-call(bf16[16,16,128]{2,1,0:T(8,128)(2,1)} %x_ref.1, bf16[2,3,3,128,128]{4,3,2,1,0:T(8,128)(2,1)} %near_ref.1, bf16[2,3,3,128,128]{4,3,2,1,0:T(8,128)(2,1)} %far_ref.1), custom_call_target="tpu_custom_call" | custom-call | tf_op jit(solution)/shard_map/pallas_call | solution.py:379
  17.3 0.6 %copy.5 = bf16[16,16,128]{2,1,0:T(8,128)(2,1)} copy(bf16[16,16,128]{2,1,0:T(8,128)(2,1)S(1)} %shard_map.37) | data formatting | bytes 131072

commit v12 on v11

--- a/solution.py
+++ b/solution.py
@@ -226,21 +226,24 @@
             jnp.maximum(total, 0.0).astype(hidden.dtype).reshape(size, span, wide)
         )
 
-    def block_out_of(n, lane, weights, start):
-        lanes = slice(lane * channels, (lane + 1) * channels)
-        shifted = [
-            hidden[pl.ds(start, half + 2 * FAR), FAR * b:FAR * b + side, lanes]
-            for b in range(3)
-        ]
-        taps = [
-            shifted[b][FAR * a:FAR * a + half].reshape(half * side, channels)
-            for a in range(3) for b in range(3)
-        ]
-        total = jnp.dot(
+    def far_sum(lanes, weights, start):
+        taps = []
+        for lane in lanes:
+            part = slice(lane * channels, (lane + 1) * channels)
+            shifted = [
+                hidden[pl.ds(start, half + 2 * FAR), FAR * b:FAR * b + side, part]
+                for b in range(3)
+            ]
+            taps += [
+                shifted[b][FAR * a:FAR * a + half].reshape(half * side, channels)
+                for a in range(3) for b in range(3)
+            ]
+        return jnp.dot(
             jnp.concatenate(taps, axis=1), weights, preferred_element_type=jnp.float32
         ).reshape(half, side, channels)
-        own = pads[n, pl.ds(HALO + start, half), body]
-        return (own.astype(jnp.float32) + total).astype(jnp.bfloat16)
+
+    def own_rows(n, start):
+        return pads[n, pl.ds(HALO + start, half), body].astype(jnp.float32)
 
     def halves_of(n, weights, half_done):
         wait_columns(n)
@@ -285,7 +288,8 @@
 
     def mirror_half(k, start):
         part = pl.ds(start, half)
-        mirror[0, part] = block_out_of(0, 0, straight(far, 0), start)
+        total = far_sum((0,), straight(far, 0), start)
+        mirror[0, part] = (own_rows(0, start) + total).astype(mirror.dtype)
 
         @pl.when(row != col)
         def _():
@@ -316,10 +320,9 @@
                 rim_start(n, (4 + which, 6 + which))
 
     def average_half(n, k, start):
-        value = average(
-            block_out_of(n, 0, straight(far, n), start),
-            block_out_of(n, 1, crossed(far, n), start),
-        )
+        weights = jnp.concatenate([straight(far, n), crossed(far, n)], axis=0)
+        total = far_sum((0, 1), weights, start)
+        value = (own_rows(n, start) + total * 0.5).astype(out_ref.dtype)
         if n == blocks - 1:
             out_ref[pl.ds(start, half)] = value
         else:

time: 18 us -> 18.1 us (level)
  no operation moved by 1% of the time
where the time goes in v12:
time: 18.1 us; the launch traced here: 17.9 us
  Pallas kernels  17.3 us (96%)
  local copies, waits for them, and re-layouts  0.63 us (3%)
    pallas_call x1, Pallas kernels, by_tiles(): pl.pallas_call(functools.partial(tile_kernel, count, side), out_shape=jax...  17.3 us
    unnamed x1, local copies, waits for them, and re-layouts  0.63 us

profile of v12, /device:TPU:1, one launch (start us, length us, event | category | flops | bytes accessed | tf_op | source)
XLA Modules:
  0.0 17.9 jit_solution(4555868683213380397)
XLA Ops:
  0.0 17.3 %shard_map.37 = bf16[16,16,128]{2,1,0:T(8,128)(2,1)S(1)} custom-call(bf16[16,16,128]{2,1,0:T(8,128)(2,1)} %x_ref.1, bf16[2,3,3,128,128]{4,3,2,1,0:T(8,128)(2,1)} %near_ref.1, bf16[2,3,3,128,128]{4,3,2,1,0:T(8,128)(2,1)} %far_ref.1), custom_call_target="tpu_custom_call" | custom-call | tf_op jit(solution)/shard_map/pallas_call | solution.py:382
  17.3 0.6 %copy.5 = bf16[16,16,128]{2,1,0:T(8,128)(2,1)} copy(bf16[16,16,128]{2,1,0:T(8,128)(2,1)S(1)} %shard_map.37) | data formatting | bytes 131072
